TPU v7x, 32 devices: a whole 2x2x4 slice. The times are simulated.
32 devices in a mesh: lat: 8 (over z, x), lon: 4 (over y, core).
Axes of the slice: x: 2, y: 2, z: 4, core: 2. Of those that a mesh axis runs over, the one named last changes fastest.
Arguments:
- fields: bfloat16 [4, 48, 48, 384], P(None, 'lat', 'lon'), may hold values from -6 to 6
- cotangent: bfloat16 [4, 48, 48, 384], P(None, 'lat', 'lon'), may hold values from -6 to 6
- window_mask: int32 [2, 8, 4], P(None, 'lat', 'lon'), may hold values 0 or 1
- mask_token: bfloat16 [384], replicated, may hold values from -4 to 4
- norm_gain: bfloat16 [384], replicated, may hold values from 0.5 to 1.5
- qkv_weight: bfloat16 [1152, 384], replicated, may hold values from -0.3125 to 0.3125
- out_weight: bfloat16 [384, 384], replicated, may hold values from -0.3125 to 0.3125
- bias_table: float32 [8, 12, 759], P('lat'), may hold values from -300 to 300
- bias_index: int32 [144, 144], replicated, may hold values from 0 to 758
Outputs:
- output: bfloat16 [4, 48, 48, 384], P(None, 'lat', 'lon')
- input_grad: bfloat16 [4, 48, 48, 384], P(None, 'lat', 'lon')
- weight_grads: float32 [1536, 384], P(('lat', 'lon'))
- table_grad: float32 [8, 12, 759], P('lat')
- vector_grads: float32 [2, 384], replicated
All inputs are finite; a program needn't handle non-finite values. No bound on the sum of `window_mask` on one device may be relied on, other than what follows from the above.
Results may differ from a plain program's by a relative error of at most 0.02.
Values may be sent and summed in bfloat16 or wider, within the bound.
A program may use at most 64 MiB of HBM per device.

v0:
```python
import jax
import jax.numpy as jnp
from jax import lax
from jax.sharding import PartitionSpec as P

HEADS = 12
HEAD_DIM = 32
WIN_Z = 2
WIN_LAT = 6
WIN_LON = 12
WIN_TOK = 144
NBIAS = 759


EPS = 1e-05
BLOCKED = -10000.0
QUERY_BLOCK = 16


def passed_along(value, axis, steps):
    count = lax.axis_size(axis)
    pairs = [(source, (source + steps) % count) for source in range(count)]
    return lax.ppermute(value, axis, pairs)


def expand_mask(window_mask):
    spread = jnp.repeat(window_mask, WIN_Z, axis=0)
    spread = jnp.repeat(spread, WIN_LAT, axis=1)
    return jnp.repeat(spread, WIN_LON, axis=2)


def region_of(coords, extent, window):
    return (coords >= extent - window).astype(jnp.int32) + (coords >= extent - window // 2).astype(
        jnp.int32
    )


def to_windows(value):
    level_count, row_count, col_count, chan_count = value.shape
    value = value.reshape(
        level_count // WIN_Z,
        WIN_Z,
        row_count // WIN_LAT,
        WIN_LAT,
        col_count // WIN_LON,
        WIN_LON,
        chan_count,
    )
    value = value.transpose(2, 0, 4, 1, 3, 5, 6)
    return value.reshape(
        row_count // WIN_LAT, level_count // WIN_Z * (col_count // WIN_LON), WIN_TOK, chan_count
    )


def from_windows(value, level_count, col_count):
    row_groups = value.shape[0]
    chan_count = value.shape[3]
    value = value.reshape(
        row_groups, level_count // WIN_Z, col_count // WIN_LON, WIN_Z, WIN_LAT, WIN_LON, chan_count
    )
    value = value.transpose(1, 3, 0, 4, 2, 5, 6)
    return value.reshape(level_count, row_groups * WIN_LAT, col_count, chan_count)


def one_hot_block(ids):
    entries = jnp.arange(NBIAS, dtype=jnp.int32)
    return (ids[:, None] == entries[None, :]).astype(jnp.float32)


def index_blocks(bias_index):
    return bias_index.reshape(WIN_TOK // QUERY_BLOCK, QUERY_BLOCK * WIN_TOK)


def lookup_bias(bias_table, bias_index):
    row_groups = bias_table.shape[0]
    flat_table = bias_table.reshape(row_groups * HEADS, NBIAS)

    def pick(ids):
        return jnp.einsum(
            "rb,nb->rn", flat_table, one_hot_block(ids), precision=lax.Precision.HIGHEST
        )

    picked = lax.map(pick, index_blocks(bias_index))
    picked = picked.transpose(1, 0, 2)
    return picked.reshape(row_groups, HEADS, WIN_TOK, WIN_TOK)


def table_sums(bias_grad, bias_index):
    row_groups = bias_grad.shape[0]
    block_count = WIN_TOK // QUERY_BLOCK
    flat_grad = bias_grad.reshape(row_groups * HEADS, block_count, QUERY_BLOCK * WIN_TOK).transpose(
        1, 0, 2
    )

    def accumulate(total, items):
        grad_block, ids = items
        return (
            total
            + jnp.einsum(
                "rn,nb->rb", grad_block, one_hot_block(ids), precision=lax.Precision.HIGHEST
            ),
            None,
        )

    start = jnp.zeros((row_groups * HEADS, NBIAS), jnp.float32)
    total, _ = lax.scan(accumulate, start, (flat_grad, index_blocks(bias_index)))
    return total.reshape(row_groups, HEADS, NBIAS)


def roll_in(first, second):
    lat_shift = WIN_LAT // 2
    lon_shift = WIN_LON // 2
    first = jnp.roll(first, -(WIN_Z // 2), axis=0)
    second = jnp.roll(second, -(WIN_Z // 2), axis=0)
    strip = passed_along(jnp.stack((first[:, :lat_shift], second[:, :lat_shift])), "lat", -1)
    first = jnp.concatenate((first[:, lat_shift:], strip[0]), axis=1)
    second = jnp.concatenate((second[:, lat_shift:], strip[1]), axis=1)
    strip = passed_along(jnp.stack((first[:, :, :lon_shift], second[:, :, :lon_shift])), "lon", -1)
    first = jnp.concatenate((first[:, :, lon_shift:], strip[0]), axis=2)
    second = jnp.concatenate((second[:, :, lon_shift:], strip[1]), axis=2)
    return (first, second)


def roll_out_one(value):
    lat_shift = WIN_LAT // 2
    lon_shift = WIN_LON // 2
    strip = passed_along(value[:, -lat_shift:], "lat", 1)
    value = jnp.concatenate((strip, value[:, :-lat_shift]), axis=1)
    strip = passed_along(value[:, :, -lon_shift:], "lon", 1)
    value = jnp.concatenate((strip, value[:, :, :-lon_shift]), axis=2)
    return jnp.roll(value, WIN_Z // 2, axis=0)


def window_block(tokens_win, cot_win, bias, regions, qkv_weight, out_weight):
    wide = jnp.float32
    low = jnp.bfloat16
    groups = tokens_win.shape[0]
    members = tokens_win.shape[1]
    scale = HEAD_DIM ** (-0.5)
    projected = jnp.einsum(
        "rmtd,fd->rmtf", tokens_win, qkv_weight, preferred_element_type=wide
    ).astype(low)
    projected = projected.reshape(groups, members, WIN_TOK, 3, HEADS, HEAD_DIM)
    queries = projected[:, :, :, 0]
    key_rows = projected[:, :, :, 1]
    values = projected[:, :, :, 2]
    scores = (
        jnp.einsum("rmthe,rmshe->rmhts", queries, key_rows, preferred_element_type=wide) * scale
        + bias[:, None]
    )
    apart = regions[:, :, :, None] != regions[:, :, None, :]
    scores = jnp.where(apart[:, :, None], BLOCKED, scores)
    row_max = jnp.max(scores, axis=-1, keepdims=True)
    exponent = jnp.exp(scores - row_max)
    attn_prob = (exponent / jnp.sum(exponent, axis=-1, keepdims=True)).astype(low)
    mixed_heads = jnp.einsum(
        "rmhts,rmshe->rmthe", attn_prob, values, preferred_element_type=wide
    ).astype(low)
    mixed_heads = mixed_heads.reshape(groups, members, WIN_TOK, HEADS * HEAD_DIM)
    branch = jnp.einsum(
        "rmtd,fd->rmtf", mixed_heads, out_weight, preferred_element_type=wide
    ).astype(low)
    out_grad = jnp.einsum("rmtf,rmtd->fd", cot_win, mixed_heads, preferred_element_type=wide)
    grad_mixed = jnp.einsum(
        "rmtf,fd->rmtd", cot_win, out_weight, preferred_element_type=wide
    ).astype(low)
    grad_mixed = grad_mixed.reshape(groups, members, WIN_TOK, HEADS, HEAD_DIM)
    grad_attn = jnp.einsum("rmthe,rmshe->rmhts", grad_mixed, values, preferred_element_type=wide)
    grad_values = jnp.einsum(
        "rmhts,rmthe->rmshe", attn_prob, grad_mixed, preferred_element_type=wide
    ).astype(low)
    prob_float = attn_prob.astype(wide)
    grad_scores = prob_float * (grad_attn - jnp.sum(prob_float * grad_attn, axis=-1, keepdims=True))
    bias_grad = jnp.sum(grad_scores, axis=1)
    scores_low = grad_scores.astype(low)
    grad_queries = (
        jnp.einsum("rmhts,rmshe->rmthe", scores_low, key_rows, preferred_element_type=wide) * scale
    ).astype(low)
    grad_keys = (
        jnp.einsum("rmhts,rmthe->rmshe", scores_low, queries, preferred_element_type=wide) * scale
    ).astype(low)
    grad_qkv = jnp.stack((grad_queries, grad_keys, grad_values), axis=3).reshape(
        groups, members, WIN_TOK, 3 * HEADS * HEAD_DIM
    )
    qkv_grad = jnp.einsum("rmtf,rmtd->fd", grad_qkv, tokens_win, preferred_element_type=wide)
    grad_tokens = jnp.einsum(
        "rmtf,fd->rmtd", grad_qkv, qkv_weight, preferred_element_type=wide
    ).astype(low)
    return (branch, grad_tokens, qkv_grad, out_grad, bias_grad)


def local(
    fields,
    cotangent,
    window_mask,
    mask_token,
    norm_gain,
    qkv_weight,
    out_weight,
    bias_table,
    bias_index,
):
    wide = jnp.float32
    level_count, row_count, col_count, chan_count = fields.shape
    masked = expand_mask(window_mask) == 1
    filled = jnp.where(masked[..., None], mask_token, fields)
    filled_wide = filled.astype(wide)
    center = filled_wide - jnp.mean(filled_wide, axis=-1, keepdims=True)
    inv_std = lax.rsqrt(jnp.mean(center * center, axis=-1, keepdims=True) + EPS)
    standard = center * inv_std
    normed = (standard * norm_gain.astype(wide)).astype(jnp.bfloat16)
    shifted, shifted_cot = roll_in(normed, cotangent)
    lat_coords = lax.axis_index("lat") * row_count + jnp.arange(row_count, dtype=jnp.int32)
    level_ids = region_of(jnp.arange(level_count, dtype=jnp.int32), level_count, WIN_Z)
    lat_ids = region_of(lat_coords, row_count * lax.axis_size("lat"), WIN_LAT)
    regions = level_ids[:, None] * 3 + lat_ids[None, :]
    region_field = jnp.broadcast_to(
        regions[:, :, None, None], (level_count, row_count, col_count, 1)
    )
    region_win = to_windows(region_field)[..., 0]
    bias = lookup_bias(bias_table, bias_index)
    branch_win, grad_win, qkv_grad, out_grad, bias_grad = window_block(
        to_windows(shifted), to_windows(shifted_cot), bias, region_win, qkv_weight, out_weight
    )
    branch_local = from_windows(branch_win, level_count, col_count)
    grad_local = from_windows(grad_win, level_count, col_count)
    branch = roll_out_one(branch_local)
    grad_normed = roll_out_one(grad_local)
    output = (filled_wide + branch.astype(wide)).astype(jnp.bfloat16)
    scaled = grad_normed.astype(wide) * norm_gain.astype(wide)
    grad_filled = cotangent.astype(wide) + inv_std * (
        scaled
        - jnp.mean(scaled, axis=-1, keepdims=True)
        - standard * jnp.mean(scaled * standard, axis=-1, keepdims=True)
    )
    input_grad = jnp.where(masked[..., None], 0.0, grad_filled).astype(jnp.bfloat16)
    gain_grad = jnp.sum(grad_normed.astype(wide) * standard, axis=(0, 1, 2))
    token_grad = jnp.sum(jnp.where(masked[..., None], grad_filled, 0.0), axis=(0, 1, 2))
    vector_grads = lax.psum(jnp.stack((gain_grad, token_grad)), ("lat", "lon"))
    table_local = table_sums(bias_grad, bias_index)
    table_grad = lax.psum(table_local.astype(jnp.bfloat16), "lon").astype(jnp.float32)
    grad_terms = jnp.concatenate((qkv_grad, out_grad), axis=0)
    weight_grads = lax.psum_scatter(grad_terms, ("lat", "lon"), scatter_dimension=0, tiled=True)
    return (output, input_grad, weight_grads, table_grad, vector_grads)


def solution(mesh):
    placed = (
        P(None, "lat", "lon", None),
        P(None, "lat", "lon", None),
        P(None, "lat", "lon"),
        P(),
        P(),
        P(),
        P(),
        P("lat", None, None),
        P(),
    )
    return jax.shard_map(
        local,
        mesh=mesh,
        in_specs=placed,
        out_specs=(
            P(None, "lat", "lon", None),
            P(None, "lat", "lon", None),
            P(("lat", "lon"), None),
            P("lat", None, None),
            P(),
        ),
        check_vma=False,
    )
```

profile of v0, /device:TPU:0, one launch (start us, length us, event | category | flops | bytes accessed | tf_op | source)
XLA Modules:
  0.0 215.7 jit_solution(16490348538443828495)
XLA Ops:
  13.7 6.0 %collective-permute-start = (bf16[2,4,3,12,384]{4,3,2,1,0:T(8,128)(2,1)}, bf16[2,4,3,12,384]{4,3,2,1,0:T(8,128)(2,1)}, u32[]{:S(2)}, u32[]{:S(2)}) collective-permute-start(bf16[2,4,3,12,384]{4,3,2,1,0:T(8,128)(2,1)} %pad_maximum_fusion.11), channel_id=1, source_target_pairs={{0,28},{4,0},{8,4},{12,8},{16,12},{20,16},{24,20},{28,24},{1,29},{... | collective-permute-start | bytes 663560 | tf_op jit(solution)/shard_map/ppermute | solution.py:23
  19.8 38.2 %while.21 = (s32[]{:T(128)}, f32[9,12,2304]{2,1,0:T(8,128)}, s32[9,2304]{1,0:T(8,128)S(1)}, f32[12,759]{1,0:T(8,128)S(1)}, s32[]{:T(128)}) while((s32[]{:T(128)}, f32[9,12,2304]{2,1,0:T(8,128)}, s32[9,2304]{1,0:T(8,128)S(1)}, f32[12,759]{1,0:T(8,128)S(1)}, s32[]{:T(128)}) %tuple.71), condition=%wide.region_3.4_spmd, body=%wide.region_2.3_spmd.sunk | while | flops 253566720 | bytes 211613 | solution.py:83
  19.9 4.2 %fusion.84 = f32[9,12,2304]{2,1,0:T(8,128)} fusion(f32[9,12,2304]{2,1,0:T(8,128)} %get-tuple-element.186, s32[]{:T(128)S(6)} %copy.121, f32[12,759]{1,0:T(8,128)S(1)} %get-tuple-element.193, s32[2304]{0:T(1024)S(1)} %dynamic-slice_reduce_fusion.4), kind=kOutput, calls=%fused_computation.4.clone.1 | convolution fusion | flops 253566720 | bytes 193108 | tf_op jit(solution)/shard_map/while/body/eval_jaxpr/rb,nb->rn/dot_general | solution.py:79
  24.1 4.2 %fusion.84 = f32[9,12,2304]{2,1,0:T(8,128)} fusion(f32[9,12,2304]{2,1,0:T(8,128)} %get-tuple-element.186, s32[]{:T(128)S(6)} %copy.121, f32[12,759]{1,0:T(8,128)S(1)} %get-tuple-element.193, s32[2304]{0:T(1024)S(1)} %dynamic-slice_reduce_fusion.4), kind=kOutput, calls=%fused_computation.4.clone.1 | convolution fusion | flops 253566720 | bytes 193108 | tf_op jit(solution)/shard_map/while/body/eval_jaxpr/rb,nb->rn/dot_general | solution.py:79
  28.4 4.2 %fusion.84 = f32[9,12,2304]{2,1,0:T(8,128)} fusion(f32[9,12,2304]{2,1,0:T(8,128)} %get-tuple-element.186, s32[]{:T(128)S(6)} %copy.121, f32[12,759]{1,0:T(8,128)S(1)} %get-tuple-element.193, s32[2304]{0:T(1024)S(1)} %dynamic-slice_reduce_fusion.4), kind=kOutput, calls=%fused_computation.4.clone.1 | convolution fusion | flops 253566720 | bytes 193108 | tf_op jit(solution)/shard_map/while/body/eval_jaxpr/rb,nb->rn/dot_general | solution.py:79
  32.6 4.2 %fusion.84 = f32[9,12,2304]{2,1,0:T(8,128)} fusion(f32[9,12,2304]{2,1,0:T(8,128)} %get-tuple-element.186, s32[]{:T(128)S(6)} %copy.121, f32[12,759]{1,0:T(8,128)S(1)} %get-tuple-element.193, s32[2304]{0:T(1024)S(1)} %dynamic-slice_reduce_fusion.4), kind=kOutput, calls=%fused_computation.4.clone.1 | convolution fusion | flops 253566720 | bytes 193108 | tf_op jit(solution)/shard_map/while/body/eval_jaxpr/rb,nb->rn/dot_general | solution.py:79
  36.8 4.2 %fusion.84 = f32[9,12,2304]{2,1,0:T(8,128)} fusion(f32[9,12,2304]{2,1,0:T(8,128)} %get-tuple-element.186, s32[]{:T(128)S(6)} %copy.121, f32[12,759]{1,0:T(8,128)S(1)} %get-tuple-element.193, s32[2304]{0:T(1024)S(1)} %dynamic-slice_reduce_fusion.4), kind=kOutput, calls=%fused_computation.4.clone.1 | convolution fusion | flops 253566720 | bytes 193108 | tf_op jit(solution)/shard_map/while/body/eval_jaxpr/rb,nb->rn/dot_general | solution.py:79
  41.1 4.2 %fusion.84 = f32[9,12,2304]{2,1,0:T(8,128)} fusion(f32[9,12,2304]{2,1,0:T(8,128)} %get-tuple-element.186, s32[]{:T(128)S(6)} %copy.121, f32[12,759]{1,0:T(8,128)S(1)} %get-tuple-element.193, s32[2304]{0:T(1024)S(1)} %dynamic-slice_reduce_fusion.4), kind=kOutput, calls=%fused_computation.4.clone.1 | convolution fusion | flops 253566720 | bytes 193108 | tf_op jit(solution)/shard_map/while/body/eval_jaxpr/rb,nb->rn/dot_general | solution.py:79
  45.3 4.2 %fusion.84 = f32[9,12,2304]{2,1,0:T(8,128)} fusion(f32[9,12,2304]{2,1,0:T(8,128)} %get-tuple-element.186, s32[]{:T(128)S(6)} %copy.121, f32[12,759]{1,0:T(8,128)S(1)} %get-tuple-element.193, s32[2304]{0:T(1024)S(1)} %dynamic-slice_reduce_fusion.4), kind=kOutput, calls=%fused_computation.4.clone.1 | convolution fusion | flops 253566720 | bytes 193108 | tf_op jit(solution)/shard_map/while/body/eval_jaxpr/rb,nb->rn/dot_general | solution.py:79
  49.6 4.2 %fusion.84 = f32[9,12,2304]{2,1,0:T(8,128)} fusion(f32[9,12,2304]{2,1,0:T(8,128)} %get-tuple-element.186, s32[]{:T(128)S(6)} %copy.121, f32[12,759]{1,0:T(8,128)S(1)} %get-tuple-element.193, s32[2304]{0:T(1024)S(1)} %dynamic-slice_reduce_fusion.4), kind=kOutput, calls=%fused_computation.4.clone.1 | convolution fusion | flops 253566720 | bytes 193108 | tf_op jit(solution)/shard_map/while/body/eval_jaxpr/rb,nb->rn/dot_general | solution.py:79
  53.8 4.2 %fusion.84 = f32[9,12,2304]{2,1,0:T(8,128)} fusion(f32[9,12,2304]{2,1,0:T(8,128)} %get-tuple-element.186, s32[]{:T(128)S(6)} %copy.121, f32[12,759]{1,0:T(8,128)S(1)} %get-tuple-element.193, s32[2304]{0:T(1024)S(1)} %dynamic-slice_reduce_fusion.4), kind=kOutput, calls=%fused_computation.4.clone.1 | convolution fusion | flops 253566720 | bytes 193108 | tf_op jit(solution)/shard_map/while/body/eval_jaxpr/rb,nb->rn/dot_general | solution.py:79
  58.0 2.0 copy.61
  60.0 2.5 %add.93 = f32[12,144,144]{2,1,0:T(8,128)} reshape(f32[12,9,2304]{2,1,0:T(8,128)S(1)} %copy.61) | data formatting | bytes 1990656 | tf_op jit(solution)/shard_map/add | solution.py:148
  62.5 3.0 %copy.62 = f32[12,144,144]{1,2,0:T(8,128)} copy(f32[12,144,144]{2,1,0:T(8,128)} %add.93) | data formatting | bytes 1990656 | tf_op jit(solution)/shard_map/add | solution.py:148
  68.1 4.1 %collective-permute-done.1 = bf16[2,4,6,6,384]{4,3,2,1,0:T(8,128)(2,1)S(1)} collective-permute-done((bf16[2,4,6,6,384]{4,3,2,1,0:T(8,128)(2,1)S(1)}, bf16[2,4,6,6,384]{4,3,2,1,0:T(8,128)(2,1)S(1)}, u32[]{:S(2)}, u32[]{:S(2)}) %collective-permute-start.1) | collective-permute-done | bytes 221216 | tf_op jit(solution)/shard_map/ppermute | solution.py:23
  74.3 4.7 %fusion.64 = (f32[2,12,144]{2,1,0:T(8,128)S(1)}, f32[2,12,144,144]{2,3,1,0:T(8,128)}) fusion(f32[12,144,144]{1,2,0:T(8,128)} %copy.62, pred[2,144,144]{1,2,0:T(8,128)(4,1)S(1)} %broadcast_compare_fusion, bf16[1,2,144,3,12,32]{2,5,4,3,1,0:T(8,128)(2,1)S(1)} %bitcast.123), kind=kOutput, calls=%fused_computation.139 | convolution fusion | flops 34338960 | bytes 3859968 | tf_op jit(solution)/shard_map/sub | solution.py:154
  79.0 2.8 %fusion.8 = (f32[2,12,144]{2,1,0:T(8,128)S(1)}, bf16[2,12,144,144]{2,3,1,0:T(8,128)(2,1)S(1)}, f32[2,12,144,144]{2,3,1,0:T(8,128)S(1)}) fusion(f32[2,12,144,144]{2,3,1,0:T(8,128)} %get-tuple-element.126, f32[2,12,144]{2,1,0:T(8,128)S(1)} %get-tuple-element.125, bf16[2,144,12,32]{1,3,2,0:T(8,128)(2,1)S(1)} %bitcast.133, ...), kind=kOutput, calls=%fused_computation.16 | convolution fusion | flops 34335360 | bytes 5809664 | tf_op jit(solution)/shard_map/rmthe,rmshe->rmhts/dot_general | solution.py:168
  82.5 2.0 fusion.10
  88.5 1.3 convolution_convert_fusion.3
  90.5 1.7 reshape_transpose_reshape.9
  92.2 1.7 fusion.61
  93.9 1.7 reshape_transpose_reshape.8
  95.6 1.7 fusion.62
  97.3 1.6 pad_maximum_fusion
  98.9 2.1 copy.74
  101.0 2.5 %reshape.254 = f32[12,9,2304]{2,1,0:T(8,128)} reshape(f32[12,144,144]{2,1,0:T(8,128)S(1)} %copy.74) | data formatting | bytes 1990656 | tf_op jit(solution)/shard_map/reshape | solution.py:91
  103.5 41.0 %while.22 = (s32[]{:T(128)}, f32[12,759]{1,0:T(8,128)S(1)}, f32[9,12,2304]{2,0,1:T(8,128)}, s32[9,2304]{1,0:T(8,128)}, s32[]{:T(128)}, /*index=5*/s32[]{:T(128)}) while((s32[]{:T(128)}, f32[12,759]{1,0:T(8,128)S(1)}, f32[9,12,2304]{2,0,1:T(8,128)}, s32[9,2304]{1,0:T(8,128)}, s32[]{:T(128)}, /*index=5*/s32[]{:T(128)}) %tuple.70), condition=%wide.region_12.13_spmd.clone, body=%wide.region_11.12_spmd.clone.sunk | while | flops 253584928 | bytes 432383 | solution.py:106
  105.7 2.3 %fusion.85 = f32[12,759]{1,0:T(8,128)S(1)} fusion(s32[2304]{0:T(1024)S(1)} %dynamic-slice_reduce_fusion.5, f32[1,12,2304]{2,0,1:T(1,128)S(1)} %constant_dynamic-slice_fusion.2, f32[12,759]{1,0:T(8,128)S(1)} %get-tuple-element.202, pred[]{:T(512)S(6)} %compare.3), kind=kOutput, calls=%fused_computation.9.clone.1 | convolution fusion | flops 253584928 | bytes 192673 | tf_op jit(solution)/shard_map/while/body/eval_jaxpr/rn,nb->rb/dot_general | solution.py:99
  109.0 1.3 constant_dynamic-slice_fusion.2
  110.3 2.3 %fusion.85 = f32[12,759]{1,0:T(8,128)S(1)} fusion(s32[2304]{0:T(1024)S(1)} %dynamic-slice_reduce_fusion.5, f32[1,12,2304]{2,0,1:T(1,128)S(1)} %constant_dynamic-slice_fusion.2, f32[12,759]{1,0:T(8,128)S(1)} %get-tuple-element.202, pred[]{:T(512)S(6)} %compare.3), kind=kOutput, calls=%fused_computation.9.clone.1 | convolution fusion | flops 253584928 | bytes 192673 | tf_op jit(solution)/shard_map/while/body/eval_jaxpr/rn,nb->rb/dot_general | solution.py:99
  113.6 1.3 constant_dynamic-slice_fusion.2
  114.8 2.3 %fusion.85 = f32[12,759]{1,0:T(8,128)S(1)} fusion(s32[2304]{0:T(1024)S(1)} %dynamic-slice_reduce_fusion.5, f32[1,12,2304]{2,0,1:T(1,128)S(1)} %constant_dynamic-slice_fusion.2, f32[12,759]{1,0:T(8,128)S(1)} %get-tuple-element.202, pred[]{:T(512)S(6)} %compare.3), kind=kOutput, calls=%fused_computation.9.clone.1 | convolution fusion | flops 253584928 | bytes 192673 | tf_op jit(solution)/shard_map/while/body/eval_jaxpr/rn,nb->rb/dot_general | solution.py:99
  118.1 1.3 constant_dynamic-slice_fusion.2
  119.4 2.3 %fusion.85 = f32[12,759]{1,0:T(8,128)S(1)} fusion(s32[2304]{0:T(1024)S(1)} %dynamic-slice_reduce_fusion.5, f32[1,12,2304]{2,0,1:T(1,128)S(1)} %constant_dynamic-slice_fusion.2, f32[12,759]{1,0:T(8,128)S(1)} %get-tuple-element.202, pred[]{:T(512)S(6)} %compare.3), kind=kOutput, calls=%fused_computation.9.clone.1 | convolution fusion | flops 253584928 | bytes 192673 | tf_op jit(solution)/shard_map/while/body/eval_jaxpr/rn,nb->rb/dot_general | solution.py:99
  122.7 1.3 constant_dynamic-slice_fusion.2
  123.9 2.3 %fusion.85 = f32[12,759]{1,0:T(8,128)S(1)} fusion(s32[2304]{0:T(1024)S(1)} %dynamic-slice_reduce_fusion.5, f32[1,12,2304]{2,0,1:T(1,128)S(1)} %constant_dynamic-slice_fusion.2, f32[12,759]{1,0:T(8,128)S(1)} %get-tuple-element.202, pred[]{:T(512)S(6)} %compare.3), kind=kOutput, calls=%fused_computation.9.clone.1 | convolution fusion | flops 253584928 | bytes 192673 | tf_op jit(solution)/shard_map/while/body/eval_jaxpr/rn,nb->rb/dot_general | solution.py:99
  127.2 1.3 constant_dynamic-slice_fusion.2
  128.5 2.3 %fusion.85 = f32[12,759]{1,0:T(8,128)S(1)} fusion(s32[2304]{0:T(1024)S(1)} %dynamic-slice_reduce_fusion.5, f32[1,12,2304]{2,0,1:T(1,128)S(1)} %constant_dynamic-slice_fusion.2, f32[12,759]{1,0:T(8,128)S(1)} %get-tuple-element.202, pred[]{:T(512)S(6)} %compare.3), kind=kOutput, calls=%fused_computation.9.clone.1 | convolution fusion | flops 253584928 | bytes 192673 | tf_op jit(solution)/shard_map/while/body/eval_jaxpr/rn,nb->rb/dot_general | solution.py:99
  131.8 1.3 constant_dynamic-slice_fusion.2
  133.0 2.3 %fusion.85 = f32[12,759]{1,0:T(8,128)S(1)} fusion(s32[2304]{0:T(1024)S(1)} %dynamic-slice_reduce_fusion.5, f32[1,12,2304]{2,0,1:T(1,128)S(1)} %constant_dynamic-slice_fusion.2, f32[12,759]{1,0:T(8,128)S(1)} %get-tuple-element.202, pred[]{:T(512)S(6)} %compare.3), kind=kOutput, calls=%fused_computation.9.clone.1 | convolution fusion | flops 253584928 | bytes 192673 | tf_op jit(solution)/shard_map/while/body/eval_jaxpr/rn,nb->rb/dot_general | solution.py:99
  136.3 1.3 constant_dynamic-slice_fusion.2
  137.6 2.3 %fusion.85 = f32[12,759]{1,0:T(8,128)S(1)} fusion(s32[2304]{0:T(1024)S(1)} %dynamic-slice_reduce_fusion.5, f32[1,12,2304]{2,0,1:T(1,128)S(1)} %constant_dynamic-slice_fusion.2, f32[12,759]{1,0:T(8,128)S(1)} %get-tuple-element.202, pred[]{:T(512)S(6)} %compare.3), kind=kOutput, calls=%fused_computation.9.clone.1 | convolution fusion | flops 253584928 | bytes 192673 | tf_op jit(solution)/shard_map/while/body/eval_jaxpr/rn,nb->rb/dot_general | solution.py:99
  142.1 2.3 %fusion.85 = f32[12,759]{1,0:T(8,128)S(1)} fusion(s32[2304]{0:T(1024)S(1)} %dynamic-slice_reduce_fusion.5, f32[1,12,2304]{2,0,1:T(1,128)S(1)} %constant_dynamic-slice_fusion.2, f32[12,759]{1,0:T(8,128)S(1)} %get-tuple-element.202, pred[]{:T(512)S(6)} %compare.3), kind=kOutput, calls=%fused_computation.9.clone.1 | convolution fusion | flops 253584928 | bytes 192673 | tf_op jit(solution)/shard_map/while/body/eval_jaxpr/rn,nb->rb/dot_general | solution.py:99
  144.5 13.5 %psum.14 = bf16[1,12,759]{2,0,1:T(2,128)(2,1)S(1)} all-reduce(bf16[1,12,759]{2,0,1:T(2,128)(2,1)S(1)} %convert_element_type.161), channel_id=1, replica_groups=mesh['lat'=8,'lon'=4] {'lon'}, use_global_device_ids=true, to_apply=%region_13.14 | all-reduce | flops 9108 | bytes 36432 | tf_op jit(solution)/shard_map/psum | solution.py:241
  161.6 2.7 %collective-permute-done.5 = bf16[4,6,6,384]{3,2,1,0:T(8,128)(2,1)S(1)} collective-permute-done((bf16[4,6,6,384]{3,2,1,0:T(8,128)(2,1)S(1)}, bf16[4,6,6,384]{3,2,1,0:T(8,128)(2,1)S(1)}, u32[]{:S(2)}, u32[]{:S(2)}) %collective-permute-start.5) | collective-permute-done | bytes 110624 | tf_op jit(solution)/shard_map/ppermute | solution.py:23
  164.3 1.4 fusion.25
  165.9 1.5 fusion.36
  169.0 39.9 %psum.15 = f32[2,384]{1,0:T(2,128)} all-reduce(f32[2,384]{1,0:T(2,128)S(1)} %pad_maximum_fusion.17), channel_id=1, replica_groups=mesh['lat'=8,'lon'=4] {'lat','lon'}, use_global_device_ids=true, to_apply=%region_16.17 | all-reduce | flops 768 | bytes 6144 | tf_op jit(solution)/shard_map/psum | solution.py:239
  (122 shorter events, 32.9 us)
Async XLA Ops:
  7.2 66.0 %copy-start = (bf16[1152,384]{1,0:T(8,128)(2,1)S(1)}, bf16[1152,384]{1,0:T(8,128)(2,1)}, u32[]{:S(2)}) copy-start(bf16[1152,384]{1,0:T(8,128)(2,1)} %param.18) | copy-start | bytes 2654212
  7.2 5.3 %copy-start.4 = (bf16[4,6,12,384]{3,0,2,1:T(4,128)(2,1)S(1)}, bf16[4,6,12,384]{3,0,2,1:T(4,128)(2,1)}, u32[]{:S(2)}) copy-start(bf16[4,6,12,384]{3,0,2,1:T(4,128)(2,1)} %param.14) | copy-start | bytes 663556
  7.2 201.6 %reduce-scatter.2.cloned.1.call-start = ((), (), s32[]{:S(2)}) async-start(), calls=%async_computation.1 | async-start | bytes 2433024 | tf_op jit(solution)/shard_map/reduce_scatter | solution.py:243
  12.4 7.2 %copy-start.11 = (s32[144,144]{1,0:T(8,128)S(1)}, s32[144,144]{1,0:T(8,128)}, u32[]{:S(2)}) copy-start(s32[144,144]{1,0:T(8,128)} %param.21) | copy-start | bytes 248836
  12.5 7.3 %copy-start.12 = (f32[1,12,759]{2,0,1:T(1,128)S(1)}, f32[1,12,759]{2,0,1:T(1,128)}, u32[]{:S(2)}) copy-start(f32[1,12,759]{2,0,1:T(1,128)} %param.20) | copy-start | bytes 109300
  13.7 52.1 %collective-permute-start = (bf16[2,4,3,12,384]{4,3,2,1,0:T(8,128)(2,1)}, bf16[2,4,3,12,384]{4,3,2,1,0:T(8,128)(2,1)}, u32[]{:S(2)}, u32[]{:S(2)}) collective-permute-start(bf16[2,4,3,12,384]{4,3,2,1,0:T(8,128)(2,1)} %pad_maximum_fusion.11), channel_id=1, source_target_pairs={{0,28},{4,0},{8,4},{12,8},{16,12},{20,16},{24,20},{28,24},{1,29},{... | collective-permute-start | bytes 663560 | tf_op jit(solution)/shard_map/ppermute | solution.py:23
  58.0 4.5 %copy-start.10 = (s32[9,2304]{1,0:T(8,128)}, s32[9,2304]{1,0:T(8,128)S(1)}, u32[]{:S(2)}) copy-start(s32[9,2304]{1,0:T(8,128)S(1)} %get-tuple-element.216) | copy-start | bytes 248836
  66.8 5.6 %copy-start.8 = (bf16[384,384]{1,0:T(8,128)(2,1)S(1)}, bf16[384,384]{1,0:T(8,128)(2,1)}, u32[]{:S(2)}) copy-start(bf16[384,384]{1,0:T(8,128)(2,1)} %param.19) | copy-start | bytes 884740
  67.1 5.2 %collective-permute-start.1 = (bf16[2,4,6,6,384]{4,3,2,1,0:T(8,128)(2,1)S(1)}, bf16[2,4,6,6,384]{4,3,2,1,0:T(8,128)(2,1)S(1)}, u32[]{:S(2)}, u32[]{:S(2)}) collective-permute-start(bf16[2,4,6,6,384]{4,3,2,1,0:T(8,128)(2,1)S(1)} %pad_maximum_fusion.12), channel_id=1, source_target_pairs={{0,3},{1,0},{2,1},{3,2},{4,7},{5,4},{6,5},{7,6},{8,11},{9,8},{10,9... | collective-permute-start | bytes 663560 | tf_op jit(solution)/shard_map/ppermute | solution.py:23
  72.4 0.7 copy-start.2
  85.6 1.0 copy-start.9
  85.6 2.0 copy-start.3
  93.9 64.8 %collective-permute-start.4 = (bf16[4,3,12,384]{3,2,1,0:T(8,128)(2,1)}, bf16[4,3,12,384]{3,2,1,0:T(8,128)(2,1)}, u32[]{:S(2)}, u32[]{:S(2)}) collective-permute-start(bf16[4,3,12,384]{3,2,1,0:T(8,128)(2,1)} %get-tuple-element.110), channel_id=1, source_target_pairs={{0,4},{4,8},{8,12},{12,16},{16,20},{20,24},{24,28},{28,0},{1,5},{5... | collective-permute-start | bytes 331784 | tf_op jit(solution)/shard_map/ppermute | solution.py:23
  97.3 62.4 %collective-permute-start.2 = (bf16[4,3,12,384]{3,2,1,0:T(8,128)(2,1)}, bf16[4,3,12,384]{3,2,1,0:T(8,128)(2,1)}, u32[]{:S(2)}, u32[]{:S(2)}) collective-permute-start(bf16[4,3,12,384]{3,2,1,0:T(8,128)(2,1)} %get-tuple-element.113), channel_id=1, source_target_pairs={{0,4},{4,8},{8,12},{12,16},{16,20},{20,24},{24,28},{28,0},{1,5},{5... | collective-permute-start | bytes 331784 | tf_op jit(solution)/shard_map/ppermute | solution.py:23
  103.5 55.2 %copy-start.7 = (bf16[4,3,12,384]{3,2,1,0:T(8,128)(2,1)S(1)}, bf16[4,3,12,384]{3,2,1,0:T(8,128)(2,1)}, u32[]{:S(2)}) copy-start(bf16[4,3,12,384]{3,2,1,0:T(8,128)(2,1)} %get-tuple-element.111) | copy-start | bytes 331780
  103.5 56.3 %copy-start.6 = (bf16[4,3,12,384]{3,2,1,0:T(8,128)(2,1)S(1)}, bf16[4,3,12,384]{3,2,1,0:T(8,128)(2,1)}, u32[]{:S(2)}) copy-start(bf16[4,3,12,384]{3,2,1,0:T(8,128)(2,1)} %get-tuple-element.112) | copy-start | bytes 331780
  103.5 60.8 %copy-start.1 = (bf16[4,6,12,384]{3,0,2,1:T(4,128)(2,1)S(1)}, bf16[4,6,12,384]{3,0,2,1:T(4,128)(2,1)}, u32[]{:S(2)}) copy-start(bf16[4,6,12,384]{3,0,2,1:T(4,128)(2,1)} %param.13) | copy-start | bytes 663556
  103.5 60.8 %copy-start.13 = (bf16[384]{0:T(512)(128)(2,1)S(1)}, bf16[384]{0:T(512)(128)(2,1)}, u32[]{:S(2)}) copy-start(bf16[384]{0:T(512)(128)(2,1)} %param.16) | copy-start | bytes 2308
  144.5 21.4 %copy-start.5 = (bf16[4,6,12,384]{3,0,2,1:T(4,128)(2,1)S(1)}, bf16[4,6,12,384]{3,0,2,1:T(4,128)(2,1)}, u32[]{:S(2)}) copy-start(bf16[4,6,12,384]{3,0,2,1:T(4,128)(2,1)} %param.14) | copy-start | bytes 663556
  159.7 4.6 %collective-permute-start.5 = (bf16[4,6,6,384]{3,2,1,0:T(8,128)(2,1)S(1)}, bf16[4,6,6,384]{3,2,1,0:T(8,128)(2,1)S(1)}, u32[]{:S(2)}, u32[]{:S(2)}) collective-permute-start(bf16[4,6,6,384]{3,2,1,0:T(8,128)(2,1)S(1)} %fusion.47), channel_id=1, source_target_pairs={{0,1},{1,2},{2,3},{3,0},{4,5},{5,6},{6,7},{7,4},{8,9},{9,10},{10,1... | collective-permute-start | bytes 331784 | tf_op jit(solution)/shard_map/ppermute | solution.py:23
  160.8 5.1 %collective-permute-start.3 = (bf16[4,6,6,384]{3,2,1,0:T(8,128)(2,1)S(1)}, bf16[4,6,6,384]{3,2,1,0:T(8,128)(2,1)S(1)}, u32[]{:S(2)}, u32[]{:S(2)}) collective-permute-start(bf16[4,6,6,384]{3,2,1,0:T(8,128)(2,1)S(1)} %fusion.48), channel_id=1, source_target_pairs={{0,1},{1,2},{2,3},{3,0},{4,5},{5,6},{6,7},{7,4},{8,9},{9,10},{10,1... | collective-permute-start | bytes 331784 | tf_op jit(solution)/shard_map/ppermute | solution.py:23
Sparse Core Ops, SparseCore 0:
  99.0 101.0 reduce-scatter.1
where the time goes:
time: 217 us; the launch traced here: 216 us
  matrix products  73 us (34%)
  blocking collectives  53.3 us (25%)
  local copies, waits for them, and re-layouts  43.9 us (20%)
  other arithmetic  15.9 us (7%)
  between operations  14.5 us (7%)
  starting transfers between devices  7.81 us (4%)
  waiting for transfers between devices  7.04 us (3%)
    psum x1, blocking collectives, local(): vector_grads = lax.psum(jnp.stack((gain_grad, token_grad)), ('lat', 'lon'))  39.9 us
    dot_general x9, matrix products, pick(): jnp.einsum('rb,nb->rn', flat_table, one_hot_block(ids), precision=lax.Pre...  37.9 us
    dot_general x9, matrix products, accumulate(): jnp.einsum('rn,nb->rb', grad_block, one_hot_block(ids), precision=lax.Pre...  21.1 us
    psum x1, blocking collectives, local(): lax.psum(table_local.astype(jnp.bfloat16), 'lon').astype(jnp.float32)  13.5 us
    dynamic_slice x9, local copies, waits for them, and re-layouts, table_sums(): lax.scan(accumulate, start, (flat_grad, index_blocks(bias_index)))  11.4 us
    dynamic_slice x18, local copies, waits for them, and re-layouts, lookup_bias(): picked = lax.map(pick, index_blocks(bias_index))  8.69 us
    ppermute x6, starting transfers between devices, passed_along(): return lax.ppermute(value, axis, pairs)  7.77 us
    ppermute x6, waiting for transfers between devices, passed_along(): return lax.ppermute(value, axis, pairs)  7.02 us
  transfers between devices with their start and end apart: 7, of which 3 were waited for; matrix products, arithmetic and copies ran while one was open for 48% of the time, Pallas kernels for 0%

commit v1 on v0

v1 whole, which is shorter than its diff:
```python
import functools

import jax
import jax.numpy as jnp
from jax import lax
from jax.experimental import pallas as pl
from jax.experimental.pallas import tpu as pltpu
from jax.sharding import PartitionSpec as P

D = 384
HEADS = 12
HEAD_DIM = 32
NBIAS = 759
EPS = 1e-05
BLOCKED = -10000.0
NEVER = -1e30

PIECE = 36
PADDED = 40
TOK = 4 * PADDED
QUAD = 2 * PADDED
CHUNKS = 6
LANES = 128
ROWS = 16

WIDE = jnp.float32
LOW = jnp.bfloat16
VMEM = pl.BlockSpec(memory_space=pltpu.VMEM)
SMEM = pl.BlockSpec(memory_space=pltpu.SMEM)
PARAMS = pltpu.CompilerParams(vmem_limit_bytes=48 * 1024 * 1024)


def nn(a, b):
    return lax.dot_general(a, b, (((1,), (0,)), ((), ())), preferred_element_type=WIDE)


def nt(a, b):
    return lax.dot_general(a, b, (((1,), (1,)), ((), ())), preferred_element_type=WIDE)


def tn(a, b):
    return lax.dot_general(a, b, (((0,), (0,)), ((), ())), preferred_element_type=WIDE)


def places():
    for level in range(4):
        shifted = (level - 1) % 4
        for row in range(6):
            yield level, row, row // 3, (shifted // 2) * PADDED + (shifted % 2) * 18 + (row % 3) * 6


def pack_kernel(mask_ref, fields_ref, cot_ref, q0, q1, q2, q3, held):
    for quad in range(4):
        for win in range(2):
            start = win * PADDED + PIECE - 4
            held[quad, start : start + 8, :] = jnp.zeros((8, 2 * D), WIDE)
    for level, row, half, start in places():
        for part, ref in enumerate((fields_ref, cot_ref)):
            value = ref[level, row].astype(WIDE)
            lanes = slice(part * D, part * D + D)
            held[2 * half, start : start + 6, lanes] = value[0:6]
            held[2 * half + 1, start : start + 6, lanes] = value[6:12]
    low = mask_ref[0, 0, 0].astype(WIDE)
    high = mask_ref[1, 0, 0].astype(WIDE)
    for quad in range(4):
        for win, (first, second) in enumerate(((low, high), (high, low))):
            start = win * PADDED + PIECE
            held[quad, start : start + 1, :] = jnp.full((1, 2 * D), first)
            held[quad, start + 1 : start + 2, :] = jnp.full((1, 2 * D), second)
    for quad, ref in enumerate((q0, q1, q2, q3)):
        ref[...] = held[quad].astype(LOW)


def unpack_kernel(q0, q1, q2, q3, output_ref, grad_ref, held):
    for quad, ref in enumerate((q0, q1, q2, q3)):
        held[quad] = ref[...].astype(WIDE)
    for level, row, half, start in places():
        for part, ref in enumerate((output_ref, grad_ref)):
            lanes = slice(part * D, part * D + D)
            left = held[2 * half, start : start + 6, lanes]
            right = held[2 * half + 1, start : start + 6, lanes]
            ref[level, row] = jnp.concatenate((left, right), axis=0).astype(LOW)


def token_of(place):
    quad = place // PADDED
    within = place % PADDED
    level = within // 18
    row = (within % 18) // 6 + (quad // 2) * 3
    col = within % 6 + (quad % 2) * 6
    return jnp.where(within < PIECE, level * 72 + row * 12 + col, -1)


def lookup_kernel(table_ref, index_ref, bias_ref, place_ref):
    rows = lax.broadcasted_iota(jnp.int32, (TOK, 144), 0)
    pick_rows = (token_of(rows) == lax.broadcasted_iota(jnp.int32, (TOK, 144), 1)).astype(WIDE).astype(LOW)
    cols = lax.broadcasted_iota(jnp.int32, (2 * LANES, 144), 0)
    cols = jnp.where(cols < TOK, token_of(cols), -1)
    pick_cols = (cols == lax.broadcasted_iota(jnp.int32, (2 * LANES, 144), 1)).astype(WIDE).astype(LOW)
    index = index_ref[...]
    high = (index >> 7).astype(WIDE).astype(LOW)
    low = (index & 127).astype(WIDE).astype(LOW)
    high = nt(nn(pick_rows, high).astype(LOW), pick_cols).astype(jnp.int32)
    low = nt(nn(pick_rows, low).astype(LOW), pick_cols).astype(jnp.int32)
    place_ref[...] = high * LANES + low
    for half in range(2):
        lanes = slice(half * LANES, half * LANES + LANES)

        def block(step, carry, lanes=lanes):
            span = pl.ds(pl.multiple_of(step * 8, 8), 8)
            place = place_ref[span, lanes]
            chunk = place >> 7
            lane = place & 127
            for head in range(HEADS):
                total = jnp.zeros((8, LANES), WIDE)
                for c in range(CHUNKS):
                    row = table_ref[head : head + 1, c * LANES : c * LANES + LANES]
                    got = jnp.take_along_axis(jnp.broadcast_to(row, (8, LANES)), lane, axis=1)
                    total = jnp.where(chunk == c, got, total)
                bias_ref[head, span, lanes] = total
            return carry

        lax.fori_loop(0, TOK // 8, block, 0)


def window_kernel(
    place_ref,
    q0,
    q1,
    q2,
    q3,
    token_ref,
    gain_ref,
    qkv_w_ref,
    out_w_ref,
    bias_ref,
    y0,
    y1,
    y2,
    y3,
    wgrad_ref,
    vgrad_ref,
    pair_ref,
    qkv_s,
    gm_s,
    mixed_s,
    gqkv_s,
):
    scale = HEAD_DIM ** (-0.5)
    pieces = [ref[...].astype(WIDE) for ref in (q0, q1, q2, q3)]

    def gathered(lanes):
        return jnp.concatenate(
            [pieces[q][w * PADDED : w * PADDED + PADDED, lanes] for w in range(2) for q in range(4)], axis=0
        )

    spot = lax.broadcasted_iota(jnp.int32, (PADDED, 1), 0)
    marks = []
    for win in range(2):
        for quad in range(4):
            start = win * PADDED + PIECE
            first = pieces[quad][start : start + 1, 0:1]
            second = pieces[quad][start + 1 : start + 2, 0:1]
            marks.append(
                jnp.where(spot < 18, first, 0.0) + jnp.where((spot >= 18) & (spot < PIECE), second, 0.0)
            )
    masked = jnp.concatenate(marks, axis=0) > 0.5
    real = (lax.broadcasted_iota(jnp.int32, (2 * TOK, 1), 0) % PADDED) < PIECE
    gain = gain_ref[...].astype(WIDE)
    filled = jnp.where(masked, token_ref[...].astype(WIDE), gathered(slice(0, D)))
    filled = jnp.where(real, filled, 0.0)
    cot_wide = jnp.where(real, gathered(slice(D, 2 * D)), 0.0)
    cot = cot_wide.astype(LOW)
    center = filled - jnp.mean(filled, axis=-1, keepdims=True)
    inv_std = lax.rsqrt(jnp.mean(center * center, axis=-1, keepdims=True) + EPS)
    standard = center * inv_std
    normed = (standard * gain).astype(LOW)
    qkv_s[...] = nt(normed, qkv_w_ref[...]).astype(LOW)
    gm_s[...] = nn(cot, out_w_ref[...]).astype(LOW)

    edge = place_ref[0] == 1
    row_at = lax.broadcasted_iota(jnp.int32, (TOK, TOK), 0)
    col_at = lax.broadcasted_iota(jnp.int32, (TOK, TOK), 1)
    pad_col = (col_at % PADDED) >= PIECE
    lat_apart = ((row_at >= TOK // 2) != (col_at >= TOK // 2)) & edge
    level_apart = ((row_at % PADDED) >= 18) != ((col_at % PADDED) >= 18)
    fills = []
    for apart in (lat_apart, lat_apart | level_apart):
        fills.append(jnp.where(pad_col, NEVER, jnp.where(apart, BLOCKED, 0.0)))
    lane_head = lax.broadcasted_iota(jnp.int32, (TOK, LANES), 1) // HEAD_DIM

    for group in range(3):
        at = group * LANES
        parts = []
        for win in range(2):
            rows = slice(win * TOK, win * TOK + TOK)
            parts.append(
                (
                    qkv_s[rows, at : at + LANES],
                    qkv_s[rows, D + at : D + at + LANES],
                    qkv_s[rows, 2 * D + at : 2 * D + at + LANES],
                    gm_s[rows, at : at + LANES],
                )
            )
        sums = [[jnp.zeros((TOK, LANES), WIDE) for _ in range(4)] for _ in range(2)]
        for member in range(4):
            head = group * 4 + member
            mine = lane_head == member
            bias = bias_ref[head, :, 0:TOK]
            pair = jnp.zeros((TOK, TOK), WIDE)
            for win in range(2):
                query, key, value, gm = parts[win]
                none = jnp.zeros_like(query)
                query = jnp.where(mine, query, none)
                value_h = jnp.where(mine, value, none)
                gm_h = jnp.where(mine, gm, none)
                key_h = jnp.where(mine, key, none)
                scores = nt(query, key) * scale + bias
                scores = jnp.where(fills[win] == 0.0, scores, fills[win])
                exponent = jnp.exp(scores - jnp.max(scores, axis=-1, keepdims=True))
                prob = (exponent / jnp.sum(exponent, axis=-1, keepdims=True)).astype(LOW)
                grad_attn = nt(gm_h, value)
                prob_wide = prob.astype(WIDE)
                weighted = prob_wide * grad_attn
                grad_scores = weighted - prob_wide * jnp.sum(weighted, axis=-1, keepdims=True)
                pair = pair + grad_scores
                low = grad_scores.astype(LOW)
                sums[win][0] += nn(prob, value_h)
                sums[win][1] += nn(low, key_h)
                sums[win][2] += tn(low, query)
                sums[win][3] += tn(prob, gm_h)
            pair_ref[head] = pair
        for win in range(2):
            rows = slice(win * TOK, win * TOK + TOK)
            mixed, gq, gk, gv = sums[win]
            mixed_s[rows, at : at + LANES] = mixed.astype(LOW)
            gqkv_s[rows, at : at + LANES] = (gq * scale).astype(LOW)
            gqkv_s[rows, D + at : D + at + LANES] = (gk * scale).astype(LOW)
            gqkv_s[rows, 2 * D + at : 2 * D + at + LANES] = gv.astype(LOW)

    mixed = mixed_s[...]
    wgrad_ref[3 * D : 4 * D, :] = tn(cot, mixed).astype(wgrad_ref.dtype)
    for part in range(3):
        wgrad_ref[part * D : part * D + D, :] = tn(gqkv_s[:, part * D : part * D + D], normed).astype(
            wgrad_ref.dtype
        )
    branch = nt(mixed, out_w_ref[...]).astype(LOW).astype(WIDE)
    output = filled + branch
    grad_normed = nn(gqkv_s[...], qkv_w_ref[...]).astype(LOW).astype(WIDE)
    scaled = grad_normed * gain
    grad_filled = cot_wide + inv_std * (
        scaled
        - jnp.mean(scaled, axis=-1, keepdims=True)
        - standard * jnp.mean(scaled * standard, axis=-1, keepdims=True)
    )
    input_grad = jnp.where(masked, 0.0, grad_filled)
    vgrad_ref[0:1, :] = jnp.sum(grad_normed * standard, axis=0, keepdims=True)
    vgrad_ref[1:2, :] = jnp.sum(jnp.where(masked, grad_filled, 0.0), axis=0, keepdims=True)
    for quad, ref in enumerate((y0, y1, y2, y3)):
        for part, value in enumerate((output, input_grad)):
            both = [value[w * TOK + quad * PADDED : w * TOK + quad * PADDED + PADDED] for w in range(2)]
            ref[:, part * D : part * D + D] = jnp.concatenate(both, axis=0).astype(LOW)


def table_kernel(pair_ref, place_ref, table_ref, turned):
    for head in range(HEADS):
        turned[:, head, :] = pair_ref[head]
    turned[:, HEADS:ROWS, :] = jnp.zeros((TOK, ROWS - HEADS, TOK), WIDE)
    lane_at = lax.broadcasted_iota(jnp.int32, (LANES, TOK), 0)

    def step(block, total):
        for inner in range(8):
            row = block * 8 + inner
            place = place_ref[pl.ds(row, 1), 0:TOK]
            chunk = place >> 7
            hot = ((place & 127) == lane_at).astype(WIDE).astype(LOW)
            grad = turned[row]
            spread = jnp.concatenate([jnp.where(chunk == c, grad, 0.0) for c in range(CHUNKS)], axis=0)
            total = total + nt(spread.astype(LOW), hot)
        return total

    total = lax.fori_loop(0, TOK // 8, step, jnp.zeros((CHUNKS * ROWS, LANES), WIDE))
    for c in range(CHUNKS):
        table_ref[:, c * LANES : c * LANES + LANES] = total[c * ROWS : c * ROWS + ROWS]


def struct(shape, dtype):
    return jax.ShapeDtypeStruct(shape, dtype)


def sent(value, lat_steps, lon_steps):
    lat_count, lon_count = lax.axis_size("lat"), lax.axis_size("lon")
    pairs = []
    for a in range(lat_count):
        for o in range(lon_count):
            to = ((a + lat_steps) % lat_count) * lon_count + (o + lon_steps) % lon_count
            pairs.append((a * lon_count + o, to))
    return lax.ppermute(value, ("lat", "lon"), pairs)


def local(
    fields,
    cotangent,
    window_mask,
    mask_token,
    norm_gain,
    qkv_weight,
    out_weight,
    bias_table,
    bias_index,
):
    quad = struct((QUAD, 2 * D), LOW)
    packed = pl.pallas_call(
        pack_kernel,
        out_shape=(quad,) * 4,
        in_specs=[SMEM, VMEM, VMEM],
        out_specs=(VMEM,) * 4,
        scratch_shapes=[pltpu.VMEM((4, QUAD, 2 * D), WIDE)],
        compiler_params=PARAMS,
        name="pack",
    )(window_mask, fields, cotangent)
    from_lon = sent(packed[2], 0, -1)
    from_lat = sent(packed[1], -1, 0)
    from_both = sent(packed[0], -1, -1)
    table = jnp.pad(bias_table[0], ((0, ROWS - HEADS), (0, CHUNKS * LANES - NBIAS)))
    bias, place = pl.pallas_call(
        lookup_kernel,
        out_shape=(struct((HEADS, TOK, 2 * LANES), WIDE), struct((TOK, 2 * LANES), jnp.int32)),
        in_specs=[VMEM, VMEM],
        out_specs=(VMEM, VMEM),
        compiler_params=PARAMS,
        cost_estimate=pl.CostEstimate(flops=4_000_000_000, bytes_accessed=8_000_000, transcendentals=0),
        name="lookup",
    )(table, bias_index)
    edge = (lax.axis_index("lat") == lax.axis_size("lat") - 1).astype(jnp.int32).reshape(1)
    y0, y1, y2, y3, wgrad, vgrad, pair = pl.pallas_call(
        window_kernel,
        out_shape=(quad,) * 4
        + (struct((4 * D, D), WIDE), struct((2, D), WIDE), struct((HEADS, TOK, TOK), WIDE)),
        in_specs=[SMEM] + [VMEM] * 9,
        out_specs=(VMEM,) * 7,
        scratch_shapes=[
            pltpu.VMEM((2 * TOK, 3 * D), LOW),
            pltpu.VMEM((2 * TOK, D), LOW),
            pltpu.VMEM((2 * TOK, D), LOW),
            pltpu.VMEM((2 * TOK, 3 * D), LOW),
        ],
        compiler_params=PARAMS,
        name="windows",
    )(
        edge,
        packed[3],
        from_lon,
        from_lat,
        from_both,
        mask_token.reshape(1, D),
        norm_gain.reshape(1, D),
        qkv_weight,
        out_weight,
        bias,
    )
    back_lon = sent(y1, 0, 1)
    back_lat = sent(y2, 1, 0)
    back_both = sent(y3, 1, 1)
    table_local = pl.pallas_call(
        table_kernel,
        out_shape=struct((ROWS, CHUNKS * LANES), WIDE),
        in_specs=[VMEM, VMEM],
        out_specs=VMEM,
        scratch_shapes=[pltpu.VMEM((TOK, ROWS, TOK), WIDE)],
        compiler_params=PARAMS,
        cost_estimate=pl.CostEstimate(flops=4_000_000_000, bytes_accessed=8_000_000, transcendentals=0),
        name="table",
    )(pair, place)
    output, input_grad = pl.pallas_call(
        unpack_kernel,
        out_shape=(struct(fields.shape, LOW), struct(fields.shape, LOW)),
        in_specs=[VMEM] * 4,
        out_specs=(VMEM, VMEM),
        scratch_shapes=[pltpu.VMEM((4, QUAD, 2 * D), WIDE)],
        compiler_params=PARAMS,
        name="unpack",
    )(back_both, back_lat, back_lon, y0)
    vector_grads = lax.psum(vgrad, ("lat", "lon"))
    table_grad = lax.psum(table_local[None, :HEADS, :NBIAS].astype(LOW), "lon").astype(WIDE)
    weight_grads = lax.psum_scatter(wgrad, ("lat", "lon"), scatter_dimension=0, tiled=True)
    return (output, input_grad, weight_grads, table_grad, vector_grads)


def solution(mesh):
    placed = (
        P(None, "lat", "lon", None),
        P(None, "lat", "lon", None),
        P(None, "lat", "lon"),
        P(),
        P(),
        P(),
        P(),
        P("lat", None, None),
        P(),
    )
    return jax.shard_map(
        local,
        mesh=mesh,
        in_specs=placed,
        out_specs=(
            P(None, "lat", "lon", None),
            P(None, "lat", "lon", None),
            P(("lat", "lon"), None),
            P("lat", None, None),
            P(),
        ),
        check_vma=False,
    )
```

time: 217 us -> 150 us (0.69)
  matrix products: 73 us -> 0 us
  local copies, waits for them, and re-layouts: 43.9 us -> 13 us
  Pallas kernels: 0 us -> 30.8 us
  waiting for transfers between devices: 7.04 us -> 32 us
  other arithmetic: 15.9 us -> 0 us
  blocking collectives: 53.3 us -> 51 us
    dot_general x29 -> x0, matrix products: 68.3 us -> none  [the longest x9 37.9 us: pick(): jnp.einsum('rb,nb->rn', flat_table, one_hot_block(ids), precision=lax.Pre...]
    reduce_scatter x1, waiting for transfers between devices: 0.01 us -> 32 us  [local(): lax.psum_scatter(wgrad, ('lat', 'lon'), scatter_dimension=0, tiled=True)]
    pallas_call x0 -> x5, Pallas kernels: none -> 30.8 us  [the longest x1 14.9 us: local(): pl.pallas_call(window_kernel, out_shape=(quad,) * 4 + (struct((4 * D, D),...]
    dynamic_slice x27 -> x0, local copies, waits for them, and re-layouts: 20.1 us -> none  [the longest x9 11.4 us: table_sums(): lax.scan(accumulate, start, (flat_grad, index_blocks(bias_index)))]
    unnamed x33 -> x41, local copies, waits for them, and re-layouts: 2.31 us -> 12.9 us
    reduce_sum x5 -> x0, other arithmetic: 7.23 us -> none  [the longest x1 2.03 us: window_block(): bias_grad = jnp.sum(grad_scores, axis=1)]
    ppermute x6, waiting for transfers between devices: 7.02 us -> 0.02 us  [sent(): return lax.ppermute(value, ('lat', 'lon'), pairs)]
    add x2 -> x0, local copies, waits for them, and re-layouts: 5.47 us -> none  [window_block(): jnp.einsum('rmthe,rmshe->rmhts', queries, key_rows, preferred_element_typ...]
  transfers between devices with their start and end apart: 7 -> 7, of which waited for: 3 -> 1; matrix products, arithmetic and copies ran while one was open for 48% -> 2% of each run, Pallas kernels for 0% -> 10%
where the time goes in v1:
time: 150 us
  blocking collectives  51 us (34%)
  waiting for transfers between devices  32 us (21%)
  Pallas kernels  30.8 us (21%)
  between operations  14.2 us (9%)
  local copies, waits for them, and re-layouts  13 us (9%)
  starting transfers between devices  9.13 us (6%)
    psum x1, blocking collectives, local(): vector_grads = lax.psum(vgrad, ('lat', 'lon'))  39.3 us
    reduce_scatter x1, waiting for transfers between devices, local(): lax.psum_scatter(wgrad, ('lat', 'lon'), scatter_dimension=0, tiled=True)  32 us
    pallas_call x1, Pallas kernels, local(): pl.pallas_call(window_kernel, out_shape=(quad,) * 4 + (struct((4 * D, D),...  14.9 us
    unnamed x41, local copies, waits for them, and re-layouts  12.9 us
    psum x1, blocking collectives, local(): lax.psum(table_local[None, :HEADS, :NBIAS].astype(LOW), 'lon').astype(WIDE)  11.7 us
    ppermute x6, starting transfers between devices, sent(): return lax.ppermute(value, ('lat', 'lon'), pairs)  9.1 us
    pallas_call x1, Pallas kernels, local(): pl.pallas_call(table_kernel, out_shape=struct((ROWS, CHUNKS * LANES), WID...  7.6 us
    pallas_call x1, Pallas kernels, local(): pl.pallas_call(lookup_kernel, out_shape=(struct((HEADS, TOK, 2 * LANES),...  6.61 us
  transfers between devices with their start and end apart: 7, of which 1 were waited for; matrix products, arithmetic and copies ran while one was open for 2% of the time, Pallas kernels for 10%

profile of v1, /device:TPU:0, one launch (start us, length us, event | category | flops | bytes accessed | tf_op | source)
XLA Modules:
  0.0 150.0 jit_solution(1893364682041988762)
XLA Ops:
  7.2 0.0 reduce-scatter.2.cloned.1.call-start
  7.2 0.7 copy.14.mask_ref
  8.0 1.0 copy.15.fields_ref
  8.9 1.0 copy.16.cot_ref
  9.9 1.4 pack.1
  11.3 2.4 %collective-permute-start = (bf16[80,768]{1,0:T(8,128)(2,1)}, bf16[80,768]{1,0:T(8,128)(2,1)S(1)}, u32[]{:S(2)}, u32[]{:S(2)}) collective-permute-start(bf16[80,768]{1,0:T(8,128)(2,1)} %get-tuple-element.21), channel_id=1, source_target_pairs={{0,3},{1,0},{2,1},{3,2},{4,7},{5,4},{6,5},{7,6},{8,11},{9,8},{10,9... | collective-permute-start | bytes 368648 | tf_op jit(solution)/shard_map/ppermute | solution.py:298
  13.7 4.5 %collective-permute-start.1 = (bf16[80,768]{1,0:T(8,128)(2,1)}, bf16[80,768]{1,0:T(8,128)(2,1)S(1)}, u32[]{:S(2)}, u32[]{:S(2)}) collective-permute-start(bf16[80,768]{1,0:T(8,128)(2,1)} %get-tuple-element.22), channel_id=1, source_target_pairs={{0,28},{1,29},{2,30},{3,31},{4,0},{5,1},{6,2},{7,3},{8,4},{9,5},{1... | collective-permute-start | bytes 368648 | tf_op jit(solution)/shard_map/ppermute | solution.py:298
  18.3 0.4 collective-permute-start.2
  18.6 0.8 copy.22
  19.4 0.0 copy-start.6
  19.4 0.9 copy-done.6
  20.3 6.6 %lookup.1 = (f32[12,160,256]{2,1,0:T(8,128)S(1)}, s32[160,256]{1,0:T(8,128)S(1)}) custom-call(f32[16,768]{1,0:T(8,128)S(1)} %pad.4.table_ref, s32[144,144]{1,0:T(8,128)S(1)} %copy-done.6), custom_call_target="tpu_custom_call" | custom-call | flops 4000000000 | bytes 8000000 | tf_op jit(solution)/shard_map/lookup/pallas_call | solution.py:326
  26.9 0.0 copy-start.13
  26.9 0.7 copy-done.13
  27.6 0.0 copy-done.15
  27.6 0.0 copy-done.16
  27.6 0.0 collective-permute-done.q1
  27.6 0.0 collective-permute-done.1.q2
  27.7 0.0 collective-permute-done.2.q3
  27.7 0.0 copy-done
  27.7 0.0 copy-done.1
  27.7 14.9 %windows.1 = (bf16[80,768]{1,0:T(8,128)(2,1)S(1)}, bf16[80,768]{1,0:T(8,128)(2,1)S(1)}, bf16[80,768]{1,0:T(8,128)(2,1)S(1)}, bf16[80,768]{1,0:T(8,128)(2,1)S(1)}...) custom-call(s32[1]{0:T(128)} %bitcast.place_ref, ...), custom_call_target="tpu_custom_call" | custom-call | tf_op jit(solution)/shard_map/windows/pallas_call | solution.py:336
  42.6 0.7 copy-done.2
  43.3 1.3 copy-done.4
  44.6 0.6 copy-done.7
  45.2 0.6 copy-done.9
  45.8 0.6 copy-done.11
  46.5 0.0 reduce-scatter.2.cloned.1.call-update
  46.5 0.9 copy-done.12
  47.4 1.4 collective-permute-start.3
  48.8 0.0 copy-done.10
  48.8 0.2 collective-permute-start.4
  48.9 0.0 copy-done.8
  48.9 0.2 collective-permute-start.5
  49.2 0.0 copy-done.5
  49.2 0.9 copy-done.14
  50.1 7.6 %table.1 = f32[16,768]{1,0:T(8,128)S(1)} custom-call(f32[12,160,160]{2,1,0:T(8,128)S(1)} %copy-done.5, s32[160,256]{1,0:T(8,128)S(1)} %copy-done.14), custom_call_target="tpu_custom_call" | custom-call | flops 4000000000 | bytes 8000000 | tf_op jit(solution)/shard_map/table/pallas_call | solution.py:365
  57.7 11.7 %psum.14 = bf16[1,12,759]{2,1,0:T(8,128)(2,1)S(1)} all-reduce(bf16[1,12,759]{2,1,0:T(8,128)(2,1)S(1)} %fusion), channel_id=1, replica_groups=mesh['lat'=8,'lon'=4] {'lon'}, use_global_device_ids=true, to_apply=%region_1.2 | all-reduce | flops 9108 | bytes 36432 | tf_op jit(solution)/shard_map/psum | solution.py:385
  69.4 0.6 copy.19
  70.1 39.3 %psum.15 = f32[2,384]{1,0:T(2,128)} all-reduce(f32[2,384]{1,0:T(2,128)S(1)} %get-tuple-element.34), channel_id=1, replica_groups=mesh['lat'=8,'lon'=4] {'lat','lon'}, use_global_device_ids=true, to_apply=%region_2.3 | all-reduce | flops 768 | bytes 6144 | tf_op jit(solution)/shard_map/psum | solution.py:384
  109.4 0.0 collective-permute-done.3.q0
  109.4 0.0 collective-permute-done.4.q1
  109.4 0.0 collective-permute-done.5.q2
  109.4 0.0 copy-done.3
  109.4 0.2 unpack.1
  109.6 0.8 copy.17
  110.4 0.8 copy.18
  111.2 32.0 %reduce-scatter.2.cloned.1.call-done = f32[48,384]{1,0:T(8,128)} async-done(((f32[1536,384]{1,0:T(8,128)}), f32[48,384]{1,0:T(8,128)}) %reduce-scatter.2.cloned.1.call-update) | async-done | bytes 73744 | tf_op jit(solution)/shard_map/reduce_scatter | solution.py:386
  (19 shorter events, 0.0 us)
Async XLA Ops:
  7.2 136.0 %reduce-scatter.2.cloned.1.call-start = ((), (), s32[]{:S(2)}) async-start(), calls=%async_computation.1 | async-start | bytes 2433024 | tf_op jit(solution)/shard_map/reduce_scatter | solution.py:386
  11.3 16.3 %collective-permute-start = (bf16[80,768]{1,0:T(8,128)(2,1)}, bf16[80,768]{1,0:T(8,128)(2,1)S(1)}, u32[]{:S(2)}, u32[]{:S(2)}) collective-permute-start(bf16[80,768]{1,0:T(8,128)(2,1)} %get-tuple-element.21), channel_id=1, source_target_pairs={{0,3},{1,0},{2,1},{3,2},{4,7},{5,4},{6,5},{7,6},{8,11},{9,8},{10,9... | collective-permute-start | bytes 368648 | tf_op jit(solution)/shard_map/ppermute | solution.py:298
  13.7 13.9 %collective-permute-start.1 = (bf16[80,768]{1,0:T(8,128)(2,1)}, bf16[80,768]{1,0:T(8,128)(2,1)S(1)}, u32[]{:S(2)}, u32[]{:S(2)}) collective-permute-start(bf16[80,768]{1,0:T(8,128)(2,1)} %get-tuple-element.22), channel_id=1, source_target_pairs={{0,28},{1,29},{2,30},{3,31},{4,0},{5,1},{6,2},{7,3},{8,4},{9,5},{1... | collective-permute-start | bytes 368648 | tf_op jit(solution)/shard_map/ppermute | solution.py:298
  18.3 9.4 %collective-permute-start.2 = (bf16[80,768]{1,0:T(8,128)(2,1)}, bf16[80,768]{1,0:T(8,128)(2,1)}, u32[]{:S(2)}, u32[]{:S(2)}) collective-permute-start(bf16[80,768]{1,0:T(8,128)(2,1)} %get-tuple-element.23), channel_id=1, source_target_pairs={{0,31},{1,28},{2,29},{3,30},{4,3},{5,0},{6,1},{7,2},{8,7},{9,4},{1... | collective-permute-start | bytes 368648 | tf_op jit(solution)/shard_map/ppermute | solution.py:298
  19.4 0.9 copy-start.6
  20.3 7.3 %copy-start.15 = (bf16[384]{0:T(512)(128)(2,1)S(1)}, bf16[384]{0:T(512)(128)(2,1)}, u32[]{:S(2)}) copy-start(bf16[384]{0:T(512)(128)(2,1)} %param.12) | copy-start | bytes 2308
  20.3 7.3 %copy-start.16 = (bf16[384]{0:T(512)(128)(2,1)S(1)}, bf16[384]{0:T(512)(128)(2,1)}, u32[]{:S(2)}) copy-start(bf16[384]{0:T(512)(128)(2,1)} %param.13) | copy-start | bytes 2308
  20.3 7.3 %copy-start = (bf16[1152,384]{1,0:T(8,128)(2,1)S(1)}, bf16[1152,384]{1,0:T(8,128)(2,1)}, u32[]{:S(2)}) copy-start(bf16[1152,384]{1,0:T(8,128)(2,1)} %qkv_w_ref.1) | copy-start | bytes 2654212
  20.3 7.4 %copy-start.1 = (bf16[384,384]{1,0:T(8,128)(2,1)S(1)}, bf16[384,384]{1,0:T(8,128)(2,1)}, u32[]{:S(2)}) copy-start(bf16[384,384]{1,0:T(8,128)(2,1)} %out_w_ref.1) | copy-start | bytes 884740
  26.9 0.7 copy-start.13
  42.6 0.7 copy-start.2
  43.3 1.3 copy-start.4
  44.6 0.6 copy-start.7
  45.2 0.7 copy-start.9
  45.8 0.6 copy-start.11
  46.5 0.9 copy-start.12
  46.5 2.3 %copy-start.10 = (bf16[80,768]{1,0:T(8,128)(2,1)S(1)}, bf16[80,768]{1,0:T(8,128)(2,1)}, u32[]{:S(2)}) copy-start(bf16[80,768]{1,0:T(8,128)(2,1)} %copy-done.9) | copy-start | bytes 368644
  46.5 2.4 %copy-start.8 = (bf16[80,768]{1,0:T(8,128)(2,1)S(1)}, bf16[80,768]{1,0:T(8,128)(2,1)}, u32[]{:S(2)}) copy-start(bf16[80,768]{1,0:T(8,128)(2,1)} %copy-done.7) | copy-start | bytes 368644
  46.5 2.7 %copy-start.5 = (f32[12,160,160]{2,1,0:T(8,128)S(1)}, f32[12,160,160]{2,1,0:T(8,128)}, u32[]{:S(2)}) copy-start(f32[12,160,160]{2,1,0:T(8,128)} %copy-done.4) | copy-start | bytes 3686404
  47.4 62.0 %collective-permute-start.3 = (bf16[80,768]{1,0:T(8,128)(2,1)S(1)}, bf16[80,768]{1,0:T(8,128)(2,1)S(1)}, u32[]{:S(2)}, u32[]{:S(2)}) collective-permute-start(bf16[80,768]{1,0:T(8,128)(2,1)S(1)} %copy-done.12), channel_id=1, source_target_pairs={{0,5},{1,6},{2,7},{3,4},{4,9},{5,10},{6,11},{7,8},{8,13},{9,14},{1... | collective-permute-start | bytes 368648 | tf_op jit(solution)/shard_map/ppermute | solution.py:298
  48.8 60.6 %collective-permute-start.4 = (bf16[80,768]{1,0:T(8,128)(2,1)S(1)}, bf16[80,768]{1,0:T(8,128)(2,1)S(1)}, u32[]{:S(2)}, u32[]{:S(2)}) collective-permute-start(bf16[80,768]{1,0:T(8,128)(2,1)S(1)} %copy-done.10), channel_id=1, source_target_pairs={{0,4},{1,5},{2,6},{3,7},{4,8},{5,9},{6,10},{7,11},{8,12},{9,13},{1... | collective-permute-start | bytes 368648 | tf_op jit(solution)/shard_map/ppermute | solution.py:298
  48.9 60.5 %collective-permute-start.5 = (bf16[80,768]{1,0:T(8,128)(2,1)S(1)}, bf16[80,768]{1,0:T(8,128)(2,1)S(1)}, u32[]{:S(2)}, u32[]{:S(2)}) collective-permute-start(bf16[80,768]{1,0:T(8,128)(2,1)S(1)} %copy-done.8), channel_id=1, source_target_pairs={{0,1},{1,2},{2,3},{3,0},{4,5},{5,6},{6,7},{7,4},{8,9},{9,10},{10,1... | collective-permute-start | bytes 368648 | tf_op jit(solution)/shard_map/ppermute | solution.py:298
  49.2 0.9 copy-start.14
  50.1 59.3 %copy-start.3 = (bf16[80,768]{1,0:T(8,128)(2,1)S(1)}, bf16[80,768]{1,0:T(8,128)(2,1)}, u32[]{:S(2)}) copy-start(bf16[80,768]{1,0:T(8,128)(2,1)} %copy-done.2) | copy-start | bytes 368644
Sparse Core Ops, SparseCore 0:
  46.7 96.4 reduce-scatter.1

commit v2 on v1

--- a/solution.py
+++ b/solution.py
@@ -69,17 +69,6 @@
             held[quad, start + 1 : start + 2, :] = jnp.full((1, 2 * D), second)
     for quad, ref in enumerate((q0, q1, q2, q3)):
         ref[...] = held[quad].astype(LOW)
-
-
-def unpack_kernel(q0, q1, q2, q3, output_ref, grad_ref, held):
-    for quad, ref in enumerate((q0, q1, q2, q3)):
-        held[quad] = ref[...].astype(WIDE)
-    for level, row, half, start in places():
-        for part, ref in enumerate((output_ref, grad_ref)):
-            lanes = slice(part * D, part * D + D)
-            left = held[2 * half, start : start + 6, lanes]
-            right = held[2 * half + 1, start : start + 6, lanes]
-            ref[level, row] = jnp.concatenate((left, right), axis=0).astype(LOW)
 
 
 def token_of(place):
@@ -254,6 +243,7 @@
         - standard * jnp.mean(scaled * standard, axis=-1, keepdims=True)
     )
     input_grad = jnp.where(masked, 0.0, grad_filled)
+    vgrad_ref[...] = jnp.zeros((8, D), WIDE)
     vgrad_ref[0:1, :] = jnp.sum(grad_normed * standard, axis=0, keepdims=True)
     vgrad_ref[1:2, :] = jnp.sum(jnp.where(masked, grad_filled, 0.0), axis=0, keepdims=True)
     for quad, ref in enumerate((y0, y1, y2, y3)):
@@ -262,7 +252,7 @@
             ref[:, part * D : part * D + D] = jnp.concatenate(both, axis=0).astype(LOW)
 
 
-def table_kernel(pair_ref, place_ref, table_ref, turned):
+def table_sums(pair_ref, place_ref, turned):
     for head in range(HEADS):
         turned[:, head, :] = pair_ref[head]
     turned[:, HEADS:ROWS, :] = jnp.zeros((TOK, ROWS - HEADS, TOK), WIDE)
@@ -279,9 +269,204 @@
             total = total + nt(spread.astype(LOW), hot)
         return total
 
-    total = lax.fori_loop(0, TOK // 8, step, jnp.zeros((CHUNKS * ROWS, LANES), WIDE))
+    return lax.fori_loop(0, TOK // 8, step, jnp.zeros((CHUNKS * ROWS, LANES), WIDE))
+
+
+def finish_kernel(
+    lat_count,
+    lon_count,
+    y0,
+    y1,
+    y2,
+    y3,
+    terms_ref,
+    vgrad_ref,
+    pair_ref,
+    place_ref,
+    output_ref,
+    grad_ref,
+    rows_ref,
+    table_ref,
+    vector_ref,
+    landed,
+    held,
+    turned,
+    pair_in,
+    pair_sum,
+    lon_in,
+    lon_sum,
+    lat_in,
+    table_in,
+    vec_in,
+    vec_sum,
+    vec_in_lat,
+    quad_send,
+    quad_recv,
+    pair_send,
+    pair_recv,
+    lon_send,
+    lon_recv,
+    lat_send,
+    lat_recv,
+    table_send,
+    table_recv,
+    vec_send,
+    vec_recv,
+    vec_lat_send,
+    vec_lat_recv,
+):
+    lat, lon = lax.axis_index("lat"), lax.axis_index("lon")
+    half = lon_count // 2
+    core, column = lon % 2, lon // 2
+
+    def lat_at(step):
+        return (lat + step + lat_count) % lat_count
+
+    def lon_at(step):
+        return (lon + step + lon_count) % lon_count
+
+    def copy(src, dst, send_sem, recv_sem, device):
+        return pltpu.make_async_remote_copy(
+            src_ref=src,
+            dst_ref=dst,
+            send_sem=send_sem,
+            recv_sem=recv_sem,
+            device_id=device,
+            device_id_type=pl.DeviceIdType.MESH,
+        )
+
+    barrier = pltpu.get_barrier_semaphore()
+    friends = [(lat, lon_at(d)) for d in range(1, lon_count)]
+    friends += [(lat_at(d), lon) for d in range(1, lat_count)]
+    friends += [(lat_at(1), lon_at(1)), (lat_at(-1), lon_at(-1))]
+    for friend in friends:
+        pl.semaphore_signal(barrier, inc=1, device_id=friend, device_id_type=pl.DeviceIdType.MESH)
+    pl.semaphore_wait(barrier, len(friends))
+
+    pair_copy = copy(
+        terms_ref.at[:, :, 1 - core], pair_in, pair_send, pair_recv, (lat, lon + 1 - 2 * core)
+    )
+    pair_copy.start()
+    quads = [
+        copy(y3, landed.at[0], quad_send.at[0], quad_recv.at[0], (lat_at(1), lon_at(1))),
+        copy(y2, landed.at[1], quad_send.at[1], quad_recv.at[1], (lat_at(1), lon)),
+        copy(y1, landed.at[2], quad_send.at[2], quad_recv.at[2], (lat, lon_at(1))),
+    ]
+    for each in quads:
+        each.start()
+    vec_in[lon] = vgrad_ref[...]
+    vecs = []
+    for d in range(1, lon_count):
+        to = lon_at(d)
+        vecs.append(copy(vgrad_ref, vec_in.at[lon], vec_send.at[to], vec_recv.at[lon], (lat, to)))
+    for each in vecs:
+        each.start()
+
+    pair_copy.wait_recv()
+
+    def add_pair(row, carry):
+        for m in range(half):
+            own = terms_ref[row, m, core].astype(WIDE)
+            pair_sum[m, row] = (own + pair_in[row, m].astype(WIDE)).astype(LOW)
+        return carry
+
+    lax.fori_loop(0, lat_count, add_pair, 0)
+
+    lon_copies = []
+    for d in range(1, half):
+        to = (column + d) % half
+        lon_copies.append(
+            copy(pair_sum.at[to], lon_in.at[column], lon_send.at[to], lon_recv.at[column], (lat, 2 * to + core))
+        )
+    for each in lon_copies:
+        each.start()
+
+    total = table_sums(pair_ref, place_ref, turned)
     for c in range(CHUNKS):
-        table_ref[:, c * LANES : c * LANES + LANES] = total[c * ROWS : c * ROWS + ROWS]
+        table_in[lon, :, c * LANES : c * LANES + LANES] = total[c * ROWS : c * ROWS + ROWS].astype(LOW)
+    tables = []
+    for d in range(1, lon_count):
+        to = lon_at(d)
+        tables.append(copy(table_in.at[lon], table_in.at[lon], table_send.at[to], table_recv.at[lon], (lat, to)))
+    for each in tables:
+        each.start()
+
+    for d in range(1, half):
+        source = (column + d) % half
+        copy(pair_sum.at[source], lon_in.at[source], lon_send.at[source], lon_recv.at[source], (lat, 2 * source + core)).wait_recv()
+
+    def add_lon(row, carry):
+        value = pair_sum[column, row].astype(WIDE)
+        for d in range(1, half):
+            value = value + lon_in[(column + d) % half, row].astype(WIDE)
+        lon_sum[row] = value.astype(LOW)
+        return carry
+
+    lax.fori_loop(0, lat_count, add_lon, 0)
+
+    lat_copies = []
+    for d in range(1, lat_count):
+        to = lat_at(d)
+        lat_copies.append(copy(lon_sum.at[to], lat_in.at[lat], lat_send.at[to], lat_recv.at[lat], (to, lon)))
+    for each in lat_copies:
+        each.start()
+
+    for d in range(1, lon_count):
+        source = lon_at(d)
+        copy(vgrad_ref, vec_in.at[source], vec_send.at[source], vec_recv.at[source], (lat, source)).wait_recv()
+    vec = vec_in[0]
+    for source in range(1, lon_count):
+        vec = vec + vec_in[source]
+    vec_sum[...] = vec
+    vec_in_lat[lat] = vec
+    vec_lats = []
+    for d in range(1, lat_count):
+        to = lat_at(d)
+        vec_lats.append(copy(vec_sum, vec_in_lat.at[lat], vec_lat_send.at[to], vec_lat_recv.at[lat], (to, lon)))
+    for each in vec_lats:
+        each.start()
+
+    for each in quads:
+        each.wait_recv()
+    for quad in range(3):
+        held[quad] = landed[quad].astype(WIDE)
+    held[3] = y0[...].astype(WIDE)
+    for level, row, part_row, start in places():
+        for part, ref in enumerate((output_ref, grad_ref)):
+            lanes = slice(part * D, part * D + D)
+            left = held[2 * part_row, start : start + 6, lanes]
+            right = held[2 * part_row + 1, start : start + 6, lanes]
+            ref[level, row] = jnp.concatenate((left, right), axis=0).astype(LOW)
+
+    for d in range(1, lon_count):
+        source = lon_at(d)
+        copy(
+            table_in.at[source], table_in.at[source], table_send.at[source], table_recv.at[source], (lat, source)
+        ).wait_recv()
+    table = table_in[0].astype(WIDE)
+    for source in range(1, lon_count):
+        table = table + table_in[source].astype(WIDE)
+    table_ref[...] = table
+
+    for d in range(1, lat_count):
+        source = lat_at(d)
+        copy(
+            vec_sum, vec_in_lat.at[source], vec_lat_send.at[source], vec_lat_recv.at[source], (source, lon)
+        ).wait_recv()
+    vec = vec_in_lat[0]
+    for source in range(1, lat_count):
+        vec = vec + vec_in_lat[source]
+    vector_ref[...] = vec
+
+    value = lon_sum[lat].astype(WIDE)
+    for d in range(1, lat_count):
+        source = lat_at(d)
+        copy(lon_sum.at[source], lat_in.at[source], lat_send.at[source], lat_recv.at[source], (source, lon)).wait_recv()
+        value = value + lat_in[source].astype(WIDE)
+    rows_ref[...] = value
+
+    for each in [pair_copy] + quads + vecs + lon_copies + tables + lat_copies + vec_lats:
+        each.wait_send()
 
 
 def struct(shape, dtype):
@@ -336,7 +521,7 @@
     y0, y1, y2, y3, wgrad, vgrad, pair = pl.pallas_call(
         window_kernel,
         out_shape=(quad,) * 4
-        + (struct((4 * D, D), WIDE), struct((2, D), WIDE), struct((HEADS, TOK, TOK), WIDE)),
+        + (struct((4 * D, D), LOW), struct((8, D), WIDE), struct((HEADS, TOK, TOK), WIDE)),
         in_specs=[SMEM] + [VMEM] * 9,
         out_specs=(VMEM,) * 7,
         scratch_shapes=[
@@ -359,31 +544,55 @@
         out_weight,
         bias,
     )
-    back_lon = sent(y1, 0, 1)
-    back_lat = sent(y2, 1, 0)
-    back_both = sent(y3, 1, 1)
-    table_local = pl.pallas_call(
-        table_kernel,
-        out_shape=struct((ROWS, CHUNKS * LANES), WIDE),
-        in_specs=[VMEM, VMEM],
-        out_specs=VMEM,
-        scratch_shapes=[pltpu.VMEM((TOK, ROWS, TOK), WIDE)],
-        compiler_params=PARAMS,
-        cost_estimate=pl.CostEstimate(flops=4_000_000_000, bytes_accessed=8_000_000, transcendentals=0),
-        name="table",
-    )(pair, place)
-    output, input_grad = pl.pallas_call(
-        unpack_kernel,
-        out_shape=(struct(fields.shape, LOW), struct(fields.shape, LOW)),
-        in_specs=[VMEM] * 4,
-        out_specs=(VMEM, VMEM),
-        scratch_shapes=[pltpu.VMEM((4, QUAD, 2 * D), WIDE)],
-        compiler_params=PARAMS,
-        name="unpack",
-    )(back_both, back_lat, back_lon, y0)
-    vector_grads = lax.psum(vgrad, ("lat", "lon"))
-    table_grad = lax.psum(table_local[None, :HEADS, :NBIAS].astype(LOW), "lon").astype(WIDE)
-    weight_grads = lax.psum_scatter(wgrad, ("lat", "lon"), scatter_dimension=0, tiled=True)
+    lat_count, lon_count = lax.axis_size("lat"), lax.axis_size("lon")
+    half = lon_count // 2
+    share = 4 * D // (lat_count * lon_count)
+    output, input_grad, weight_grads, table_full, vector_full = pl.pallas_call(
+        functools.partial(finish_kernel, lat_count, lon_count),
+        out_shape=(
+            struct(fields.shape, LOW),
+            struct(fields.shape, LOW),
+            struct((share, D), WIDE),
+            struct((ROWS, CHUNKS * LANES), WIDE),
+            struct((8, D), WIDE),
+        ),
+        in_specs=[VMEM] * 8,
+        out_specs=(VMEM,) * 5,
+        scratch_shapes=[
+            pltpu.VMEM((3, QUAD, 2 * D), LOW),
+            pltpu.VMEM((4, QUAD, 2 * D), WIDE),
+            pltpu.VMEM((TOK, ROWS, TOK), WIDE),
+            pltpu.VMEM((lat_count, half, share, D), LOW),
+            pltpu.VMEM((half, lat_count, share, D), LOW),
+            pltpu.VMEM((half, lat_count, share, D), LOW),
+            pltpu.VMEM((lat_count, share, D), LOW),
+            pltpu.VMEM((lat_count, share, D), LOW),
+            pltpu.VMEM((lon_count, ROWS, CHUNKS * LANES), LOW),
+            pltpu.VMEM((lon_count, 8, D), WIDE),
+            pltpu.VMEM((8, D), WIDE),
+            pltpu.VMEM((lat_count, 8, D), WIDE),
+            pltpu.SemaphoreType.DMA((3,)),
+            pltpu.SemaphoreType.DMA((3,)),
+            pltpu.SemaphoreType.DMA,
+            pltpu.SemaphoreType.DMA,
+            pltpu.SemaphoreType.DMA((half,)),
+            pltpu.SemaphoreType.DMA((half,)),
+            pltpu.SemaphoreType.DMA((lat_count,)),
+            pltpu.SemaphoreType.DMA((lat_count,)),
+            pltpu.SemaphoreType.DMA((lon_count,)),
+            pltpu.SemaphoreType.DMA((lon_count,)),
+            pltpu.SemaphoreType.DMA((lon_count,)),
+            pltpu.SemaphoreType.DMA((lon_count,)),
+            pltpu.SemaphoreType.DMA((lat_count,)),
+            pltpu.SemaphoreType.DMA((lat_count,)),
+        ],
+        compiler_params=pltpu.CompilerParams(
+            collective_id=0, has_side_effects=True, vmem_limit_bytes=48 * 1024 * 1024
+        ),
+        name="finish",
+    )(y0, y1, y2, y3, wgrad.reshape(lat_count, half, 2, share, D), vgrad, pair, place)
+    table_grad = table_full[None, :HEADS, :NBIAS]
+    vector_grads = vector_full[:2]
     return (output, input_grad, weight_grads, table_grad, vector_grads)
 
 

time: 150 us -> 64.3 us (0.43)
  blocking collectives: 51 us -> 0 us
  waiting for transfers between devices: 32 us -> 0.01 us
  Pallas kernels: 30.8 us -> 46.7 us
  between operations: 14.2 us -> 0.74 us
  local copies, waits for them, and re-layouts: 13 us -> 9.15 us
  starting transfers between devices: 9.13 us -> 7.35 us
    psum x2 -> x0, blocking collectives: 51 us -> none  [the longest x1 39.3 us: local(): vector_grads = lax.psum(vgrad, ('lat', 'lon'))]
    reduce_scatter x1 -> x0, waiting for transfers between devices: 32 us -> none  [local(): lax.psum_scatter(wgrad, ('lat', 'lon'), scatter_dimension=0, tiled=True)]
    pallas_call x2 -> x1, Pallas kernels: 7.8 us -> 24.5 us  [local(): pl.pallas_call(functools.partial(finish_kernel, lat_count, lon_count), ou...]
    unnamed x41 -> x20, local copies, waits for them, and re-layouts: 12.9 us -> 8.55 us
    ppermute x6 -> x3, starting transfers between devices: 9.1 us -> 7.35 us  [sent(): return lax.ppermute(value, ('lat', 'lon'), pairs)]
  transfers between devices with their start and end apart: 7 -> 3, of which waited for: 1 -> 0; matrix products, arithmetic and copies ran while one was open for 2% -> 1% of each run, Pallas kernels for 10% -> 10%
where the time goes in v2:
time: 64.3 us; the launch traced here: 64 us
  Pallas kernels  46.7 us (73%)
  local copies, waits for them, and re-layouts  9.15 us (14%)
  starting transfers between devices  7.35 us (11%)
  between operations  0.74 us (1%)
    pallas_call x1, Pallas kernels, local(): pl.pallas_call(functools.partial(finish_kernel, lat_count, lon_count), ou...  24.5 us
    pallas_call x1, Pallas kernels, local(): pl.pallas_call(window_kernel, out_shape=(quad,) * 4 + (struct((4 * D, D),...  14.9 us
    unnamed x20, local copies, waits for them, and re-layouts  8.55 us
    ppermute x3, starting transfers between devices, sent(): return lax.ppermute(value, ('lat', 'lon'), pairs)  7.35 us
    pallas_call x1, Pallas kernels, local(): pl.pallas_call(lookup_kernel, out_shape=(struct((HEADS, TOK, 2 * LANES),...  6.61 us
  transfers between devices with their start and end apart: 3, of which 0 were waited for; matrix products, arithmetic and copies ran while one was open for 1% of the time, Pallas kernels for 10%

profile of v2, /device:TPU:0, one launch (start us, length us, event | category | flops | bytes accessed | tf_op | source)
XLA Modules:
  0.0 64.0 jit_solution(18085621452019162628)
XLA Ops:
  0.6 0.7 %copy.14.mask_ref = s32[2,1,1]{2,1,0:T(1,128)S(1)} copy(s32[2,1,1]{0,2,1:T(1,128)} %param.11) | data formatting | bytes 16 | tf_op args[2]
  1.4 1.0 %copy.15.fields_ref = bf16[4,6,12,384]{3,2,1,0:T(8,128)(2,1)S(1)} copy(bf16[4,6,12,384]{3,0,2,1:T(4,128)(2,1)} %param.9) | data formatting | bytes 442368 | tf_op args[0]
  2.3 1.0 %copy.16.cot_ref = bf16[4,6,12,384]{3,2,1,0:T(8,128)(2,1)S(1)} copy(bf16[4,6,12,384]{3,0,2,1:T(4,128)(2,1)} %param.10) | data formatting | bytes 442368 | tf_op args[1]
  3.3 0.7 %pack.1 = (bf16[80,768]{1,0:T(8,128)(2,1)S(1)}, bf16[80,768]{1,0:T(8,128)(2,1)S(1)}, bf16[80,768]{1,0:T(8,128)(2,1)S(1)}, bf16[80,768]{1,0:T(8,128)(2,1)S(1)}) custom-call(s32[2,1,1]{2,1,0:T(1,128)S(1)} %copy.14.mask_ref, bf16[4,6,12,384]{3,2,1,0:T(8,128)(2,1)S(1)} %copy.15.fields_ref, bf16[4,6,12,384]{3,2,1,0:T(8,128)(2,1)S(1)} %copy.16.cot_ref), custom_call_target="tpu_custom_call" | custom-call | tf_op jit(solution)/shard_map/pack/pallas_call | solution.py:498
  4.1 2.5 %collective-permute-start = (bf16[80,768]{1,0:T(8,128)(2,1)S(1)}, bf16[80,768]{1,0:T(8,128)(2,1)S(1)}, u32[]{:S(2)}, u32[]{:S(2)}) collective-permute-start(bf16[80,768]{1,0:T(8,128)(2,1)S(1)} %get-tuple-element.24), channel_id=1, source_target_pairs={{0,3},{1,0},{2,1},{3,2},{4,7},{5,4},{6,5},{7,6},{8,11},{9,8},{10,9... | collective-permute-start | bytes 368648 | tf_op jit(solution)/shard_map/ppermute | solution.py:483
  6.5 4.5 %collective-permute-start.1 = (bf16[80,768]{1,0:T(8,128)(2,1)S(1)}, bf16[80,768]{1,0:T(8,128)(2,1)S(1)}, u32[]{:S(2)}, u32[]{:S(2)}) collective-permute-start(bf16[80,768]{1,0:T(8,128)(2,1)S(1)} %get-tuple-element.25), channel_id=1, source_target_pairs={{0,28},{1,29},{2,30},{3,31},{4,0},{5,1},{6,2},{7,3},{8,4},{9,5},{1... | collective-permute-start | bytes 368648 | tf_op jit(solution)/shard_map/ppermute | solution.py:483
  11.1 0.4 collective-permute-start.2
  11.4 0.8 %copy.22 = f32[1,12,759]{2,1,0:T(8,128)S(1)} copy(f32[1,12,759]{2,0,1:T(1,128)} %param.16) | data formatting | bytes 72864
  12.2 0.0 copy-start.3
  12.2 0.9 %copy-done.3 = s32[144,144]{1,0:T(8,128)S(1)} copy-done((s32[144,144]{1,0:T(8,128)S(1)}, s32[144,144]{1,0:T(8,128)}, u32[]{:S(2)}) %copy-start.3) | copy-done | bytes 82968
  13.1 0.0 copy-start.4
  13.1 0.0 copy-start.5
  13.1 0.0 copy-start.1
  13.1 0.0 copy-start.2
  13.1 6.6 %lookup.1 = (f32[12,160,256]{2,1,0:T(8,128)S(1)}, s32[160,256]{1,0:T(8,128)S(1)}) custom-call(f32[16,768]{1,0:T(8,128)S(1)} %pad.4.table_ref, s32[144,144]{1,0:T(8,128)S(1)} %copy-done.3), custom_call_target="tpu_custom_call" | custom-call | flops 4000000000 | bytes 8000000 | tf_op jit(solution)/shard_map/lookup/pallas_call | solution.py:511
  19.7 0.0 copy-start
  19.8 1.3 %copy-done = f32[12,160,256]{2,1,0:T(8,128)} copy-done((f32[12,160,256]{2,1,0:T(8,128)}, f32[12,160,256]{2,1,0:T(8,128)S(1)}, u32[]{:S(2)}) %copy-start) | copy-done | bytes 1966104
  21.0 0.0 copy-done.4
  21.0 0.0 copy-done.5
  21.1 0.0 collective-permute-done.q1
  21.1 0.0 collective-permute-done.1.q2
  21.1 0.0 collective-permute-done.2.q3
  21.1 0.0 copy-done.1
  21.1 0.0 copy-done.2
  21.1 14.9 %windows.1 = (bf16[80,768]{1,0:T(8,128)(2,1)S(1)}, bf16[80,768]{1,0:T(8,128)(2,1)S(1)}, bf16[80,768]{1,0:T(8,128)(2,1)S(1)}, bf16[80,768]{1,0:T(8,128)(2,1)S(1)}...) custom-call(s32[1]{0:T(128)} %bitcast.place_ref, ...), custom_call_target="tpu_custom_call" | custom-call | tf_op jit(solution)/shard_map/windows/pallas_call | solution.py:521
  36.0 24.5 %finish.1 = (bf16[4,6,12,384]{3,2,1,0:T(8,128)(2,1)S(1)}, bf16[4,6,12,384]{3,2,1,0:T(8,128)(2,1)S(1)}, f32[48,384]{1,0:T(8,128)S(1)}, f32[16,768]{1,0:T(8,128)S(1)}, f32[8,384]{1,0:T(8,128)S(1)}) custom-call(bf16[80,768]{1,0:T(8,128)(2,1)S(1)} %get-tuple-element.28.y0, bf16[80,768]{1,0:T(8,128)(2,1)S(1)} %get-tuple-element.29.y1, ...), custom_call_target="tpu_custom_call" | custom-call | tf_op jit(solution)/shard_map/finish/pallas_call | solution.py:550
  60.5 0.8 %copy.17 = bf16[4,6,12,384]{3,0,2,1:T(4,128)(2,1)} copy(bf16[4,6,12,384]{3,2,1,0:T(8,128)(2,1)S(1)} %get-tuple-element.41) | data formatting | bytes 442368
  61.3 0.6 slice.7
  61.9 0.7 %copy.19 = f32[1,12,759]{2,0,1:T(1,128)} copy(f32[1,12,759]{2,1,0:T(8,128)S(1)} %slice_bitcast_fusion) | data formatting | bytes 72864
  62.6 0.8 %copy.18 = bf16[4,6,12,384]{3,0,2,1:T(4,128)(2,1)} copy(bf16[4,6,12,384]{3,2,1,0:T(8,128)(2,1)S(1)} %get-tuple-element.42) | data formatting | bytes 442368
  63.4 0.6 copy.24
  (4 shorter events, 0.0 us)
Async XLA Ops:
  4.1 17.0 %collective-permute-start = (bf16[80,768]{1,0:T(8,128)(2,1)S(1)}, bf16[80,768]{1,0:T(8,128)(2,1)S(1)}, u32[]{:S(2)}, u32[]{:S(2)}) collective-permute-start(bf16[80,768]{1,0:T(8,128)(2,1)S(1)} %get-tuple-element.24), channel_id=1, source_target_pairs={{0,3},{1,0},{2,1},{3,2},{4,7},{5,4},{6,5},{7,6},{8,11},{9,8},{10,9... | collective-permute-start | bytes 368648 | tf_op jit(solution)/shard_map/ppermute | solution.py:483
  6.5 14.5 %collective-permute-start.1 = (bf16[80,768]{1,0:T(8,128)(2,1)S(1)}, bf16[80,768]{1,0:T(8,128)(2,1)S(1)}, u32[]{:S(2)}, u32[]{:S(2)}) collective-permute-start(bf16[80,768]{1,0:T(8,128)(2,1)S(1)} %get-tuple-element.25), channel_id=1, source_target_pairs={{0,28},{1,29},{2,30},{3,31},{4,0},{5,1},{6,2},{7,3},{8,4},{9,5},{1... | collective-permute-start | bytes 368648 | tf_op jit(solution)/shard_map/ppermute | solution.py:483
  11.1 10.0 %collective-permute-start.2 = (bf16[80,768]{1,0:T(8,128)(2,1)S(1)}, bf16[80,768]{1,0:T(8,128)(2,1)S(1)}, u32[]{:S(2)}, u32[]{:S(2)}) collective-permute-start(bf16[80,768]{1,0:T(8,128)(2,1)S(1)} %get-tuple-element.26), channel_id=1, source_target_pairs={{0,31},{1,28},{2,29},{3,30},{4,3},{5,0},{6,1},{7,2},{8,7},{9,4},{1... | collective-permute-start | bytes 368648 | tf_op jit(solution)/shard_map/ppermute | solution.py:483
  12.2 0.9 %copy-start.3 = (s32[144,144]{1,0:T(8,128)S(1)}, s32[144,144]{1,0:T(8,128)}, u32[]{:S(2)}) copy-start(s32[144,144]{1,0:T(8,128)} %index_ref.1) | copy-start | bytes 248836
  13.1 7.9 %copy-start.4 = (bf16[384]{0:T(512)(128)(2,1)S(1)}, bf16[384]{0:T(512)(128)(2,1)}, u32[]{:S(2)}) copy-start(bf16[384]{0:T(512)(128)(2,1)} %param.12) | copy-start | bytes 2308
  13.1 7.9 %copy-start.5 = (bf16[384]{0:T(512)(128)(2,1)S(1)}, bf16[384]{0:T(512)(128)(2,1)}, u32[]{:S(2)}) copy-start(bf16[384]{0:T(512)(128)(2,1)} %param.13) | copy-start | bytes 2308
  13.1 8.0 %copy-start.1 = (bf16[1152,384]{1,0:T(8,128)(2,1)S(1)}, bf16[1152,384]{1,0:T(8,128)(2,1)}, u32[]{:S(2)}) copy-start(bf16[1152,384]{1,0:T(8,128)(2,1)} %qkv_w_ref.1) | copy-start | bytes 2654212
  13.1 8.0 %copy-start.2 = (bf16[384,384]{1,0:T(8,128)(2,1)S(1)}, bf16[384,384]{1,0:T(8,128)(2,1)}, u32[]{:S(2)}) copy-start(bf16[384,384]{1,0:T(8,128)(2,1)} %out_w_ref.1) | copy-start | bytes 884740
  19.7 1.3 %copy-start = (f32[12,160,256]{2,1,0:T(8,128)}, f32[12,160,256]{2,1,0:T(8,128)S(1)}, u32[]{:S(2)}) copy-start(f32[12,160,256]{2,1,0:T(8,128)S(1)} %get-tuple-element.27.bias_ref) | copy-start | bytes 5898244

commit v3 on v2

--- a/solution.py
+++ b/solution.py
@@ -27,7 +27,7 @@
 LOW = jnp.bfloat16
 VMEM = pl.BlockSpec(memory_space=pltpu.VMEM)
 SMEM = pl.BlockSpec(memory_space=pltpu.SMEM)
-PARAMS = pltpu.CompilerParams(vmem_limit_bytes=48 * 1024 * 1024)
+PARAMS = pltpu.CompilerParams(vmem_limit_bytes=32 * 1024 * 1024)
 
 
 def nn(a, b):
@@ -47,28 +47,6 @@
         shifted = (level - 1) % 4
         for row in range(6):
             yield level, row, row // 3, (shifted // 2) * PADDED + (shifted % 2) * 18 + (row % 3) * 6
-
-
-def pack_kernel(mask_ref, fields_ref, cot_ref, q0, q1, q2, q3, held):
-    for quad in range(4):
-        for win in range(2):
-            start = win * PADDED + PIECE - 4
-            held[quad, start : start + 8, :] = jnp.zeros((8, 2 * D), WIDE)
-    for level, row, half, start in places():
-        for part, ref in enumerate((fields_ref, cot_ref)):
-            value = ref[level, row].astype(WIDE)
-            lanes = slice(part * D, part * D + D)
-            held[2 * half, start : start + 6, lanes] = value[0:6]
-            held[2 * half + 1, start : start + 6, lanes] = value[6:12]
-    low = mask_ref[0, 0, 0].astype(WIDE)
-    high = mask_ref[1, 0, 0].astype(WIDE)
-    for quad in range(4):
-        for win, (first, second) in enumerate(((low, high), (high, low))):
-            start = win * PADDED + PIECE
-            held[quad, start : start + 1, :] = jnp.full((1, 2 * D), first)
-            held[quad, start + 1 : start + 2, :] = jnp.full((1, 2 * D), second)
-    for quad, ref in enumerate((q0, q1, q2, q3)):
-        ref[...] = held[quad].astype(LOW)
 
 
 def token_of(place):
@@ -80,7 +58,49 @@
     return jnp.where(within < PIECE, level * 72 + row * 12 + col, -1)
 
 
-def lookup_kernel(table_ref, index_ref, bias_ref, place_ref):
+def pack(mask_ref, fields_ref, cot_ref, spread, held):
+    for quad in range(4):
+        for win in range(2):
+            start = win * PADDED + PIECE - 4
+            held[quad, start : start + 8, :] = jnp.zeros((8, 2 * D), WIDE)
+    for part, ref in enumerate((fields_ref, cot_ref)):
+        for row in range(6):
+            for col in range(12):
+                start = (row * 12 + col) * 4
+                value = ref[row, col].astype(WIDE)
+                for c in range(3):
+                    spread[part, c, start : start + 4, :] = value[:, c * LANES : c * LANES + LANES]
+        for level, row, half, start in places():
+            for side in range(2):
+                base = (row * 12 + side * 6) * 4 + level
+                for c in range(3):
+                    lanes = slice(part * D + c * LANES, part * D + c * LANES + LANES)
+                    held[2 * half + side, start : start + 6, lanes] = spread[part, c, pl.ds(base, 6, stride=4), :]
+    low = mask_ref[0, 0, 0].astype(WIDE)
+    high = mask_ref[0, 0, 1].astype(WIDE)
+    for quad in range(4):
+        for win, (first, second) in enumerate(((low, high), (high, low))):
+            start = win * PADDED + PIECE
+            held[quad, start : start + 1, :] = jnp.full((1, 2 * D), first)
+            held[quad, start + 1 : start + 2, :] = jnp.full((1, 2 * D), second)
+
+
+def unpack(held, spread, output_ref, grad_ref):
+    for part, ref in enumerate((output_ref, grad_ref)):
+        for level, row, half, start in places():
+            for side in range(2):
+                base = (row * 12 + side * 6) * 4 + level
+                for c in range(3):
+                    lanes = slice(part * D + c * LANES, part * D + c * LANES + LANES)
+                    spread[part, c, pl.ds(base, 6, stride=4), :] = held[2 * half + side, start : start + 6, lanes]
+        for row in range(6):
+            for col in range(12):
+                start = (row * 12 + col) * 4
+                value = [spread[part, c, start : start + 4, :] for c in range(3)]
+                ref[row, col] = jnp.concatenate(value, axis=1).astype(LOW)
+
+
+def lookup(table_ref, index_ref, bias_ref, place_ref, packed_ref):
     rows = lax.broadcasted_iota(jnp.int32, (TOK, 144), 0)
     pick_rows = (token_of(rows) == lax.broadcasted_iota(jnp.int32, (TOK, 144), 1)).astype(WIDE).astype(LOW)
     cols = lax.broadcasted_iota(jnp.int32, (2 * LANES, 144), 0)
@@ -92,24 +112,103 @@
     high = nt(nn(pick_rows, high).astype(LOW), pick_cols).astype(jnp.int32)
     low = nt(nn(pick_rows, low).astype(LOW), pick_cols).astype(jnp.int32)
     place_ref[...] = high * LANES + low
-    for half in range(2):
-        lanes = slice(half * LANES, half * LANES + LANES)
-
-        def block(step, carry, lanes=lanes):
-            span = pl.ds(pl.multiple_of(step * 8, 8), 8)
-            place = place_ref[span, lanes]
-            chunk = place >> 7
-            lane = place & 127
-            for head in range(HEADS):
-                total = jnp.zeros((8, LANES), WIDE)
-                for c in range(CHUNKS):
-                    row = table_ref[head : head + 1, c * LANES : c * LANES + LANES]
-                    got = jnp.take_along_axis(jnp.broadcast_to(row, (8, LANES)), lane, axis=1)
-                    total = jnp.where(chunk == c, got, total)
-                bias_ref[head, span, lanes] = total
-            return carry
-
-        lax.fori_loop(0, TOK // 8, block, 0)
+    for k in range(4):
+        packed_ref[:, 32 * k : 32 * k + 32] = place_ref[PADDED * k : PADDED * k + PADDED, LANES : LANES + 32]
+
+    def found(place, head):
+        chunk = place >> 7
+        lane = place & 127
+        total = jnp.zeros((8, LANES), WIDE)
+        for c in range(CHUNKS):
+            row = table_ref[head : head + 1, c * LANES : c * LANES + LANES]
+            got = jnp.take_along_axis(jnp.broadcast_to(row, (8, LANES)), lane, axis=1)
+            total = jnp.where(chunk == c, got, total)
+        return total
+
+    def block(step, carry):
+        span = pl.ds(pl.multiple_of(step * 8, 8), 8)
+        place = place_ref[span, 0:LANES]
+        for head in range(HEADS):
+            bias_ref[head, span, 0:LANES] = found(place, head)
+        return carry
+
+    lax.fori_loop(0, TOK // 8, block, 0)
+
+    def tail(step, carry):
+        place = packed_ref[pl.ds(pl.multiple_of(step * 8, 8), 8), :]
+        for head in range(HEADS):
+            total = found(place, head)
+            for k in range(4):
+                span = pl.ds(pl.multiple_of(PADDED * k + step * 8, 8), 8)
+                bias_ref[head, span, LANES : LANES + 32] = total[:, 32 * k : 32 * k + 32]
+        return carry
+
+    lax.fori_loop(0, PADDED // 8, tail, 0)
+
+
+def remote(src, dst, send_sem, recv_sem, device):
+    return pltpu.make_async_remote_copy(
+        src_ref=src,
+        dst_ref=dst,
+        send_sem=send_sem,
+        recv_sem=recv_sem,
+        device_id=device,
+        device_id_type=pl.DeviceIdType.MESH,
+    )
+
+
+def enter_kernel(
+    lat_count,
+    lon_count,
+    mask_ref,
+    fields_ref,
+    cot_ref,
+    table_ref,
+    index_ref,
+    q0,
+    q1,
+    q2,
+    q3,
+    bias_ref,
+    place_ref,
+    spread,
+    held,
+    leaving,
+    landed,
+    table,
+    packed_ref,
+    send_sem,
+    recv_sem,
+):
+    lat, lon = lax.axis_index("lat"), lax.axis_index("lon")
+    before_lat = (lat - 1 + lat_count) % lat_count
+    before_lon = (lon - 1 + lon_count) % lon_count
+    after_lat = (lat + 1) % lat_count
+    after_lon = (lon + 1) % lon_count
+    barrier = pltpu.get_barrier_semaphore()
+    friends = [(before_lat, before_lon), (before_lat, lon), (lat, before_lon)]
+    friends += [(after_lat, after_lon), (after_lat, lon), (lat, after_lon)]
+    for friend in friends:
+        pl.semaphore_signal(barrier, inc=1, device_id=friend, device_id_type=pl.DeviceIdType.MESH)
+    pack(mask_ref, fields_ref, cot_ref, spread, held)
+    for quad in range(3):
+        leaving[quad] = held[quad].astype(LOW)
+    q0[...] = held[3].astype(LOW)
+    pl.semaphore_wait(barrier, len(friends))
+    copies = [
+        remote(leaving.at[i], landed.at[i], send_sem.at[i], recv_sem.at[i], friends[i]) for i in range(3)
+    ]
+    for each in copies:
+        each.start()
+    table[...] = jnp.zeros_like(table)
+    for head in range(HEADS):
+        table[head : head + 1, 0:NBIAS] = table_ref[head]
+    lookup(table, index_ref, bias_ref, place_ref, packed_ref)
+    for each in copies:
+        each.wait()
+    q3[...] = landed[0]
+    q2[...] = landed[1]
+    q1[...] = landed[2]
 
 
 def window_kernel(
@@ -290,6 +389,7 @@
     vector_ref,
     landed,
     held,
+    spread,
     turned,
     pair_in,
     pair_sum,
@@ -325,16 +425,6 @@
     def lon_at(step):
         return (lon + step + lon_count) % lon_count
 
-    def copy(src, dst, send_sem, recv_sem, device):
-        return pltpu.make_async_remote_copy(
-            src_ref=src,
-            dst_ref=dst,
-            send_sem=send_sem,
-            recv_sem=recv_sem,
-            device_id=device,
-            device_id_type=pl.DeviceIdType.MESH,
-        )
-
     barrier = pltpu.get_barrier_semaphore()
     friends = [(lat, lon_at(d)) for d in range(1, lon_count)]
     friends += [(lat_at(d), lon) for d in range(1, lat_count)]
@@ -343,14 +433,14 @@
         pl.semaphore_signal(barrier, inc=1, device_id=friend, device_id_type=pl.DeviceIdType.MESH)
     pl.semaphore_wait(barrier, len(friends))
 
-    pair_copy = copy(
+    pair_copy = remote(
         terms_ref.at[:, :, 1 - core], pair_in, pair_send, pair_recv, (lat, lon + 1 - 2 * core)
     )
     pair_copy.start()
     quads = [
-        copy(y3, landed.at[0], quad_send.at[0], quad_recv.at[0], (lat_at(1), lon_at(1))),
-        copy(y2, landed.at[1], quad_send.at[1], quad_recv.at[1], (lat_at(1), lon)),
-        copy(y1, landed.at[2], quad_send.at[2], quad_recv.at[2], (lat, lon_at(1))),
+        remote(y3, landed.at[0], quad_send.at[0], quad_recv.at[0], (lat_at(1), lon_at(1))),
+        remote(y2, landed.at[1], quad_send.at[1], quad_recv.at[1], (lat_at(1), lon)),
+        remote(y1, landed.at[2], quad_send.at[2], quad_recv.at[2], (lat, lon_at(1))),
     ]
     for each in quads:
         each.start()
@@ -358,7 +448,7 @@
     vecs = []
     for d in range(1, lon_count):
         to = lon_at(d)
-        vecs.append(copy(vgrad_ref, vec_in.at[lon], vec_send.at[to], vec_recv.at[lon], (lat, to)))
+        vecs.append(remote(vgrad_ref, vec_in.at[lon], vec_send.at[to], vec_recv.at[lon], (lat, to)))
     for each in vecs:
         each.start()
 
@@ -376,7 +466,7 @@
     for d in range(1, half):
         to = (column + d) % half
         lon_copies.append(
-            copy(pair_sum.at[to], lon_in.at[column], lon_send.at[to], lon_recv.at[column], (lat, 2 * to + core))
+            remote(pair_sum.at[to], lon_in.at[column], lon_send.at[to], lon_recv.at[column], (lat, 2 * to + core))
         )
     for each in lon_copies:
         each.start()
@@ -387,13 +477,13 @@
     tables = []
     for d in range(1, lon_count):
         to = lon_at(d)
-        tables.append(copy(table_in.at[lon], table_in.at[lon], table_send.at[to], table_recv.at[lon], (lat, to)))
+        tables.append(remote(table_in.at[lon], table_in.at[lon], table_send.at[to], table_recv.at[lon], (lat, to)))
     for each in tables:
         each.start()
 
     for d in range(1, half):
         source = (column + d) % half
-        copy(pair_sum.at[source], lon_in.at[source], lon_send.at[source], lon_recv.at[source], (lat, 2 * source + core)).wait_recv()
+        remote(pair_sum.at[source], lon_in.at[source], lon_send.at[source], lon_recv.at[source], (lat, 2 * source + core)).wait_recv()
 
     def add_lon(row, carry):
         value = pair_sum[column, row].astype(WIDE)
@@ -407,13 +497,13 @@
     lat_copies = []
     for d in range(1, lat_count):
         to = lat_at(d)
-        lat_copies.append(copy(lon_sum.at[to], lat_in.at[lat], lat_send.at[to], lat_recv.at[lat], (to, lon)))
+        lat_copies.append(remote(lon_sum.at[to], lat_in.at[lat], lat_send.at[to], lat_recv.at[lat], (to, lon)))
     for each in lat_copies:
         each.start()
 
     for d in range(1, lon_count):
         source = lon_at(d)
-        copy(vgrad_ref, vec_in.at[source], vec_send.at[source], vec_recv.at[source], (lat, source)).wait_recv()
+        remote(vgrad_ref, vec_in.at[source], vec_send.at[source], vec_recv.at[source], (lat, source)).wait_recv()
     vec = vec_in[0]
     for source in range(1, lon_count):
         vec = vec + vec_in[source]
@@ -422,7 +512,7 @@
     vec_lats = []
     for d in range(1, lat_count):
         to = lat_at(d)
-        vec_lats.append(copy(vec_sum, vec_in_lat.at[lat], vec_lat_send.at[to], vec_lat_recv.at[lat], (to, lon)))
+        vec_lats.append(remote(vec_sum, vec_in_lat.at[lat], vec_lat_send.at[to], vec_lat_recv.at[lat], (to, lon)))
     for each in vec_lats:
         each.start()
 
@@ -431,37 +521,33 @@
     for quad in range(3):
         held[quad] = landed[quad].astype(WIDE)
     held[3] = y0[...].astype(WIDE)
-    for level, row, part_row, start in places():
-        for part, ref in enumerate((output_ref, grad_ref)):
-            lanes = slice(part * D, part * D + D)
-            left = held[2 * part_row, start : start + 6, lanes]
-            right = held[2 * part_row + 1, start : start + 6, lanes]
-            ref[level, row] = jnp.concatenate((left, right), axis=0).astype(LOW)
+    unpack(held, spread, output_ref, grad_ref)
 
     for d in range(1, lon_count):
         source = lon_at(d)
-        copy(
+        remote(
             table_in.at[source], table_in.at[source], table_send.at[source], table_recv.at[source], (lat, source)
         ).wait_recv()
     table = table_in[0].astype(WIDE)
     for source in range(1, lon_count):
         table = table + table_in[source].astype(WIDE)
-    table_ref[...] = table
+    for head in range(HEADS):
+        table_ref[head] = table[head : head + 1, 0:NBIAS]
 
     for d in range(1, lat_count):
         source = lat_at(d)
-        copy(
+        remote(
             vec_sum, vec_in_lat.at[source], vec_lat_send.at[source], vec_lat_recv.at[source], (source, lon)
         ).wait_recv()
     vec = vec_in_lat[0]
     for source in range(1, lat_count):
         vec = vec + vec_in_lat[source]
-    vector_ref[...] = vec
+    vector_ref[...] = vec[0:2]
 
     value = lon_sum[lat].astype(WIDE)
     for d in range(1, lat_count):
         source = lat_at(d)
-        copy(lon_sum.at[source], lat_in.at[source], lat_send.at[source], lat_recv.at[source], (source, lon)).wait_recv()
+        remote(lon_sum.at[source], lat_in.at[source], lat_send.at[source], lat_recv.at[source], (source, lon)).wait_recv()
         value = value + lat_in[source].astype(WIDE)
     rows_ref[...] = value
 
@@ -471,16 +557,6 @@
 
 def struct(shape, dtype):
     return jax.ShapeDtypeStruct(shape, dtype)
-
-
-def sent(value, lat_steps, lon_steps):
-    lat_count, lon_count = lax.axis_size("lat"), lax.axis_size("lon")
-    pairs = []
-    for a in range(lat_count):
-        for o in range(lon_count):
-            to = ((a + lat_steps) % lat_count) * lon_count + (o + lon_steps) % lon_count
-            pairs.append((a * lon_count + o, to))
-    return lax.ppermute(value, ("lat", "lon"), pairs)
 
 
 def local(
@@ -495,28 +571,34 @@
     bias_index,
 ):
     quad = struct((QUAD, 2 * D), LOW)
-    packed = pl.pallas_call(
-        pack_kernel,
-        out_shape=(quad,) * 4,
-        in_specs=[SMEM, VMEM, VMEM],
-        out_specs=(VMEM,) * 4,
-        scratch_shapes=[pltpu.VMEM((4, QUAD, 2 * D), WIDE)],
-        compiler_params=PARAMS,
-        name="pack",
-    )(window_mask, fields, cotangent)
-    from_lon = sent(packed[2], 0, -1)
-    from_lat = sent(packed[1], -1, 0)
-    from_both = sent(packed[0], -1, -1)
-    table = jnp.pad(bias_table[0], ((0, ROWS - HEADS), (0, CHUNKS * LANES - NBIAS)))
-    bias, place = pl.pallas_call(
-        lookup_kernel,
-        out_shape=(struct((HEADS, TOK, 2 * LANES), WIDE), struct((TOK, 2 * LANES), jnp.int32)),
-        in_specs=[VMEM, VMEM],
-        out_specs=(VMEM, VMEM),
-        compiler_params=PARAMS,
-        cost_estimate=pl.CostEstimate(flops=4_000_000_000, bytes_accessed=8_000_000, transcendentals=0),
-        name="lookup",
-    )(table, bias_index)
+    lat_count, lon_count = lax.axis_size("lat"), lax.axis_size("lon")
+    q0, q1, q2, q3, bias, place = pl.pallas_call(
+        functools.partial(enter_kernel, lat_count, lon_count),
+        out_shape=(quad,) * 4
+        + (struct((HEADS, TOK, 2 * LANES), WIDE), struct((TOK, 2 * LANES), jnp.int32)),
+        in_specs=[SMEM] + [VMEM] * 4,
+        out_specs=(VMEM,) * 6,
+        scratch_shapes=[
+            pltpu.VMEM((2, 3, 288, LANES), WIDE),
+            pltpu.VMEM((4, QUAD, 2 * D), WIDE),
+            pltpu.VMEM((3, QUAD, 2 * D), LOW),
+            pltpu.VMEM((3, QUAD, 2 * D), LOW),
+            pltpu.VMEM((ROWS, CHUNKS * LANES), WIDE),
+            pltpu.VMEM((PADDED, LANES), jnp.int32),
+            pltpu.SemaphoreType.DMA((3,)),
+            pltpu.SemaphoreType.DMA((3,)),
+        ],
+        compiler_params=pltpu.CompilerParams(
+            collective_id=1, has_side_effects=True, vmem_limit_bytes=32 * 1024 * 1024
+        ),
+        name="enter",
+    )(
+        window_mask.transpose(1, 2, 0),
+        fields.transpose(1, 2, 0, 3),
+        cotangent.transpose(1, 2, 0, 3),
+        bias_table.transpose(1, 0, 2),
+        bias_index,
+    )
     edge = (lax.axis_index("lat") == lax.axis_size("lat") - 1).astype(jnp.int32).reshape(1)
     y0, y1, y2, y3, wgrad, vgrad, pair = pl.pallas_call(
         window_kernel,
@@ -534,33 +616,33 @@
         name="windows",
     )(
         edge,
-        packed[3],
-        from_lon,
-        from_lat,
-        from_both,
+        q0,
+        q1,
+        q2,
+        q3,
         mask_token.reshape(1, D),
         norm_gain.reshape(1, D),
         qkv_weight,
         out_weight,
         bias,
     )
-    lat_count, lon_count = lax.axis_size("lat"), lax.axis_size("lon")
     half = lon_count // 2
     share = 4 * D // (lat_count * lon_count)
-    output, input_grad, weight_grads, table_full, vector_full = pl.pallas_call(
+    output, input_grad, weight_grads, table_grad, vector_grads = pl.pallas_call(
         functools.partial(finish_kernel, lat_count, lon_count),
         out_shape=(
-            struct(fields.shape, LOW),
-            struct(fields.shape, LOW),
+            struct((6, 12, 4, D), LOW),
+            struct((6, 12, 4, D), LOW),
             struct((share, D), WIDE),
-            struct((ROWS, CHUNKS * LANES), WIDE),
-            struct((8, D), WIDE),
+            struct((HEADS, 1, NBIAS), WIDE),
+            struct((2, D), WIDE),
         ),
         in_specs=[VMEM] * 8,
         out_specs=(VMEM,) * 5,
         scratch_shapes=[
             pltpu.VMEM((3, QUAD, 2 * D), LOW),
             pltpu.VMEM((4, QUAD, 2 * D), WIDE),
+            pltpu.VMEM((2, 3, 288, LANES), WIDE),
             pltpu.VMEM((TOK, ROWS, TOK), WIDE),
             pltpu.VMEM((lat_count, half, share, D), LOW),
             pltpu.VMEM((half, lat_count, share, D), LOW),
@@ -587,12 +669,13 @@
             pltpu.SemaphoreType.DMA((lat_count,)),
         ],
         compiler_params=pltpu.CompilerParams(
-            collective_id=0, has_side_effects=True, vmem_limit_bytes=48 * 1024 * 1024
+            collective_id=0, has_side_effects=True, vmem_limit_bytes=32 * 1024 * 1024
         ),
         name="finish",
     )(y0, y1, y2, y3, wgrad.reshape(lat_count, half, 2, share, D), vgrad, pair, place)
-    table_grad = table_full[None, :HEADS, :NBIAS]
-    vector_grads = vector_full[:2]
+    output = output.transpose(2, 0, 1, 3)
+    input_grad = input_grad.transpose(2, 0, 1, 3)
+    table_grad = table_grad.transpose(1, 0, 2)
     return (output, input_grad, weight_grads, table_grad, vector_grads)
 
 

time: 64.3 us -> 64.3 us (level)
  starting transfers between devices: 7.35 us -> 0 us
  Pallas kernels: 46.7 us -> 52.4 us
  local copies, waits for them, and re-layouts: 9.15 us -> 10.9 us
    ppermute x3 -> x0, starting transfers between devices: 7.35 us -> none  [sent(): return lax.ppermute(value, ('lat', 'lon'), pairs)]
    pallas_call x2 -> x1, Pallas kernels: 7.34 us -> 12.4 us  [local(): pl.pallas_call(functools.partial(enter_kernel, lat_count, lon_count), out...]
    pallas_call x1, Pallas kernels: 24.5 us -> 26.5 us  [local(): pl.pallas_call(functools.partial(finish_kernel, lat_count, lon_count), ou...]
    pallas_call x1, Pallas kernels: 14.9 us -> 13.4 us  [local(): pl.pallas_call(window_kernel, out_shape=(quad,) * 4 + (struct((4 * D, D),...]
    unnamed x20 -> x19, local copies, waits for them, and re-layouts: 8.55 us -> 9.52 us
    reshape x1, local copies, waits for them, and re-layouts: 0.01 us -> 0.68 us  [local(): mask_token.reshape(1, D)]
    reshape x1, local copies, waits for them, and re-layouts: 0.01 us -> 0.68 us  [local(): norm_gain.reshape(1, D)]
  transfers between devices with their start and end apart: 3 -> 0, of which waited for: 0 -> 0; matrix products, arithmetic and copies ran while one was open for 1% -> 0% of each run, Pallas kernels for 10% -> 0%
where the time goes in v3:
time: 64.3 us; the launch traced here: 64 us
  Pallas kernels  52.4 us (81%)
  local copies, waits for them, and re-layouts  10.9 us (17%)
  between operations  0.68 us (1%)
    pallas_call x1, Pallas kernels, local(): pl.pallas_call(functools.partial(finish_kernel, lat_count, lon_count), ou...  26.5 us
    pallas_call x1, Pallas kernels, local(): pl.pallas_call(window_kernel, out_shape=(quad,) * 4 + (struct((4 * D, D),...  13.4 us
    pallas_call x1, Pallas kernels, local(): pl.pallas_call(functools.partial(enter_kernel, lat_count, lon_count), out...  12.4 us
    unnamed x19, local copies, waits for them, and re-layouts  9.52 us

profile of v3, /device:TPU:0, one launch (start us, length us, event | category | flops | bytes accessed | tf_op | source)
XLA Modules:
  0.0 64.0 jit_solution(16962093824394936126)
XLA Ops:
  0.6 0.7 %reshape.26.token_ref = bf16[1,384]{1,0:T(2,128)(2,1)S(1)} reshape(bf16[384]{0:T(512)(128)(2,1)} %param.12) | data formatting | bytes 1536 | tf_op jit(solution)/shard_map/reshape | solution.py:623
  1.3 0.7 %reshape.27.gain_ref = bf16[1,384]{1,0:T(2,128)(2,1)S(1)} reshape(bf16[384]{0:T(512)(128)(2,1)} %param.13) | data formatting | bytes 1536 | tf_op jit(solution)/shard_map/reshape | solution.py:624
  2.0 0.0 copy-start.2
  2.0 0.9 %copy-done.2 = bf16[4,6,12,384]{3,0,2,1:T(4,128)(2,1)S(1)} copy-done((bf16[4,6,12,384]{3,0,2,1:T(4,128)(2,1)S(1)}, bf16[4,6,12,384]{3,0,2,1:T(4,128)(2,1)}, u32[]{:S(2)}) %copy-start.2) | copy-done | bytes 221208
  2.9 0.0 copy-start.3
  2.9 0.9 %copy-done.3 = bf16[4,6,12,384]{3,0,2,1:T(4,128)(2,1)S(1)} copy-done((bf16[4,6,12,384]{3,0,2,1:T(4,128)(2,1)S(1)}, bf16[4,6,12,384]{3,0,2,1:T(4,128)(2,1)}, u32[]{:S(2)}) %copy-start.3) | copy-done | bytes 221208
  3.9 0.0 copy-start.4
  3.9 0.9 %copy-done.4 = s32[144,144]{1,0:T(8,128)S(1)} copy-done((s32[144,144]{1,0:T(8,128)S(1)}, s32[144,144]{1,0:T(8,128)}, u32[]{:S(2)}) %copy-start.4) | copy-done | bytes 82968
  4.8 0.0 copy-start.5
  4.8 0.8 %copy-done.5 = f32[1,12,759]{2,0,1:T(1,128)S(1)} copy-done((f32[1,12,759]{2,0,1:T(1,128)S(1)}, f32[1,12,759]{2,0,1:T(1,128)}, u32[]{:S(2)}) %copy-start.5) | copy-done | bytes 36456
  5.6 0.0 copy-start.6
  5.6 0.7 %copy-done.6 = s32[2,1,1]{0,2,1:T(1,128)S(1)} copy-done((s32[2,1,1]{0,2,1:T(1,128)S(1)}, s32[2,1,1]{0,2,1:T(1,128)}, u32[]{:S(2)}) %copy-start.6) | copy-done | bytes 32
  6.2 12.4 %enter.1 = (bf16[80,768]{1,0:T(8,128)(2,1)S(1)}, bf16[80,768]{1,0:T(8,128)(2,1)S(1)}, bf16[80,768]{1,0:T(8,128)(2,1)S(1)}, bf16[80,768]{1,0:T(8,128)(2,1)S(1)}, ...) custom-call(s32[1,1,2]{2,1,0:T(1,128)S(1)} %bitcast.16, bf16[6,12,4,384]{3,2,1,0:T(4,128)(2,1)S(1)} %bitcast.12, ...), custom_call_target="tpu_custom_call" | custom-call | tf_op jit(solution)/shard_map/enter/pallas_call | solution.py:575
  18.6 0.0 copy-start
  18.7 1.2 %copy-done = bf16[1152,384]{1,0:T(8,128)(2,1)S(1)} copy-done((bf16[1152,384]{1,0:T(8,128)(2,1)S(1)}, bf16[1152,384]{1,0:T(8,128)(2,1)}, u32[]{:S(2)}) %copy-start) | copy-done | bytes 884760
  19.8 0.0 copy-start.1
  19.8 1.0 %copy-done.1 = bf16[384,384]{1,0:T(8,128)(2,1)S(1)} copy-done((bf16[384,384]{1,0:T(8,128)(2,1)S(1)}, bf16[384,384]{1,0:T(8,128)(2,1)}, u32[]{:S(2)}) %copy-start.1) | copy-done | bytes 294936
  20.8 13.4 %windows.1 = (bf16[80,768]{1,0:T(8,128)(2,1)S(1)}, bf16[80,768]{1,0:T(8,128)(2,1)S(1)}, bf16[80,768]{1,0:T(8,128)(2,1)S(1)}, bf16[80,768]{1,0:T(8,128)(2,1)S(1)}...) custom-call(s32[1]{0:T(128)} %bitcast.place_ref, ...), custom_call_target="tpu_custom_call" | custom-call | tf_op jit(solution)/shard_map/windows/pallas_call | solution.py:603
  34.2 26.5 %finish.1 = (bf16[6,12,4,384]{3,2,1,0:T(4,128)(2,1)S(1)}, bf16[6,12,4,384]{3,2,1,0:T(4,128)(2,1)S(1)}, f32[48,384]{1,0:T(8,128)S(1)}, f32[12,1,759]{2,1,0:T(1,128)S(1)}, f32[2,384]{1,0:T(2,128)S(1)}) custom-call(bf16[80,768]{1,0:T(8,128)(2,1)S(1)} %get-tuple-element.28.y0, bf16[80,768]{1,0:T(8,128)(2,1)S(1)} %get-tuple-element.29.y1, ...), custom_call_target="tpu_custom_call" | custom-call | tf_op jit(solution)/shard_map/finish/pallas_call | solution.py:631
  60.8 0.7 %copy.19 = bf16[4,6,12,384]{3,0,2,1:T(4,128)(2,1)} copy(bf16[4,6,12,384]{3,0,2,1:T(4,128)(2,1)S(1)} %bitcast.11) | data formatting | bytes 442368
  61.4 0.7 %copy.20 = bf16[4,6,12,384]{3,0,2,1:T(4,128)(2,1)} copy(bf16[4,6,12,384]{3,0,2,1:T(4,128)(2,1)S(1)} %bitcast.10) | data formatting | bytes 442368
  62.1 0.6 copy.21
  62.8 0.6 copy.22
  63.4 0.6 copy.23
Async XLA Ops:
  2.0 0.9 %copy-start.2 = (bf16[4,6,12,384]{3,0,2,1:T(4,128)(2,1)S(1)}, bf16[4,6,12,384]{3,0,2,1:T(4,128)(2,1)}, u32[]{:S(2)}) copy-start(bf16[4,6,12,384]{3,0,2,1:T(4,128)(2,1)} %param.9) | copy-start | bytes 663556
  2.9 0.9 %copy-start.3 = (bf16[4,6,12,384]{3,0,2,1:T(4,128)(2,1)S(1)}, bf16[4,6,12,384]{3,0,2,1:T(4,128)(2,1)}, u32[]{:S(2)}) copy-start(bf16[4,6,12,384]{3,0,2,1:T(4,128)(2,1)} %param.10) | copy-start | bytes 663556
  3.9 0.9 %copy-start.4 = (s32[144,144]{1,0:T(8,128)S(1)}, s32[144,144]{1,0:T(8,128)}, u32[]{:S(2)}) copy-start(s32[144,144]{1,0:T(8,128)} %index_ref.1) | copy-start | bytes 248836
  4.8 0.8 %copy-start.5 = (f32[1,12,759]{2,0,1:T(1,128)S(1)}, f32[1,12,759]{2,0,1:T(1,128)}, u32[]{:S(2)}) copy-start(f32[1,12,759]{2,0,1:T(1,128)} %param.16) | copy-start | bytes 109300
  5.6 0.7 %copy-start.6 = (s32[2,1,1]{0,2,1:T(1,128)S(1)}, s32[2,1,1]{0,2,1:T(1,128)}, u32[]{:S(2)}) copy-start(s32[2,1,1]{0,2,1:T(1,128)} %param.11) | copy-start | bytes 28
  18.6 1.2 %copy-start = (bf16[1152,384]{1,0:T(8,128)(2,1)S(1)}, bf16[1152,384]{1,0:T(8,128)(2,1)}, u32[]{:S(2)}) copy-start(bf16[1152,384]{1,0:T(8,128)(2,1)} %qkv_w_ref.1) | copy-start | bytes 2654212
  19.8 1.0 %copy-start.1 = (bf16[384,384]{1,0:T(8,128)(2,1)S(1)}, bf16[384,384]{1,0:T(8,128)(2,1)}, u32[]{:S(2)}) copy-start(bf16[384,384]{1,0:T(8,128)(2,1)} %out_w_ref.1) | copy-start | bytes 884740

commit v4 on v3

--- a/solution.py
+++ b/solution.py
@@ -27,7 +27,9 @@
 LOW = jnp.bfloat16
 VMEM = pl.BlockSpec(memory_space=pltpu.VMEM)
 SMEM = pl.BlockSpec(memory_space=pltpu.SMEM)
-PARAMS = pltpu.CompilerParams(vmem_limit_bytes=32 * 1024 * 1024)
+HBM = pl.BlockSpec(memory_space=pltpu.HBM)
+LIMIT = 60 * 1024 * 1024
+PARAMS = pltpu.CompilerParams(vmem_limit_bytes=64 * 1024 * 1024)
 
 
 def nn(a, b):
@@ -157,18 +159,14 @@
     )
 
 
-def enter_kernel(
-    lat_count,
-    lon_count,
+def enter(
+    friends,
+    loads,
     mask_ref,
     fields_ref,
     cot_ref,
     table_ref,
     index_ref,
-    q0,
-    q1,
-    q2,
-    q3,
     bias_ref,
     place_ref,
     spread,
@@ -179,40 +177,39 @@
     packed_ref,
     send_sem,
     recv_sem,
+    greeted,
 ):
-    lat, lon = lax.axis_index("lat"), lax.axis_index("lon")
-    before_lat = (lat - 1 + lat_count) % lat_count
-    before_lon = (lon - 1 + lon_count) % lon_count
-    after_lat = (lat + 1) % lat_count
-    after_lon = (lon + 1) % lon_count
-    barrier = pltpu.get_barrier_semaphore()
-    friends = [(before_lat, before_lon), (before_lat, lon), (lat, before_lon)]
-    friends += [(after_lat, after_lon), (after_lat, lon), (lat, after_lon)]
-    for friend in friends:
-        pl.semaphore_signal(barrier, inc=1, device_id=friend, device_id_type=pl.DeviceIdType.MESH)
+    loads[0].wait()
+    loads[1].wait()
     pack(mask_ref, fields_ref, cot_ref, spread, held)
     for quad in range(3):
         leaving[quad] = held[quad].astype(LOW)
-    q0[...] = held[3].astype(LOW)
-    pl.semaphore_wait(barrier, len(friends))
+    leaving[3] = held[3].astype(LOW)
+    greeted()
     copies = [
         remote(leaving.at[i], landed.at[i], send_sem.at[i], recv_sem.at[i], friends[i]) for i in range(3)
     ]
     for each in copies:
         each.start()
+    loads[2].wait()
+    loads[3].wait()
     table[...] = jnp.zeros_like(table)
     for head in range(HEADS):
         table[head : head + 1, 0:NBIAS] = table_ref[head]
     lookup(table, index_ref, bias_ref, place_ref, packed_ref)
     for each in copies:
-        each.wait()
-    q3[...] = landed[0]
-    q2[...] = landed[1]
-    q1[...] = landed[2]
-
-
-def window_kernel(
-    place_ref,
+        each.wait_recv()
+    return copies
+
+
+def position(lat, lat_count):
+    return (lat // 2 + lat) % 2 * (lat_count // 2) + lat // 2
+
+
+def attend(
+    lat_count,
+    lon_count,
+    edge,
     q0,
     q1,
     q2,
@@ -254,8 +251,8 @@
             )
     masked = jnp.concatenate(marks, axis=0) > 0.5
     real = (lax.broadcasted_iota(jnp.int32, (2 * TOK, 1), 0) % PADDED) < PIECE
-    gain = gain_ref[...].astype(WIDE)
-    filled = jnp.where(masked, token_ref[...].astype(WIDE), gathered(slice(0, D)))
+    gain = gain_ref[...].astype(WIDE).reshape(1, D)
+    filled = jnp.where(masked, token_ref[...].astype(WIDE).reshape(1, D), gathered(slice(0, D)))
     filled = jnp.where(real, filled, 0.0)
     cot_wide = jnp.where(real, gathered(slice(D, 2 * D)), 0.0)
     cot = cot_wide.astype(LOW)
@@ -266,7 +263,6 @@
     qkv_s[...] = nt(normed, qkv_w_ref[...]).astype(LOW)
     gm_s[...] = nn(cot, out_w_ref[...]).astype(LOW)
 
-    edge = place_ref[0] == 1
     row_at = lax.broadcasted_iota(jnp.int32, (TOK, TOK), 0)
     col_at = lax.broadcasted_iota(jnp.int32, (TOK, TOK), 1)
     pad_col = (col_at % PADDED) >= PIECE
@@ -327,11 +323,15 @@
             gqkv_s[rows, 2 * D + at : 2 * D + at + LANES] = gv.astype(LOW)
 
     mixed = mixed_s[...]
-    wgrad_ref[3 * D : 4 * D, :] = tn(cot, mixed).astype(wgrad_ref.dtype)
-    for part in range(3):
-        wgrad_ref[part * D : part * D + D, :] = tn(gqkv_s[:, part * D : part * D + D], normed).astype(
-            wgrad_ref.dtype
-        )
+    band = 4 * D // lat_count
+    share = band // lon_count
+    for part in range(4):
+        value = tn(cot, mixed) if part == 3 else tn(gqkv_s[:, part * D : part * D + D], normed)
+        for i in range(lat_count // 4):
+            at = position(part * (lat_count // 4) + i, lat_count)
+            for n in range(lon_count):
+                first = i * band + n * share
+                wgrad_ref[at, n // 2, n % 2] = value[first : first + share].astype(LOW)
     branch = nt(mixed, out_w_ref[...]).astype(LOW).astype(WIDE)
     output = filled + branch
     grad_normed = nn(gqkv_s[...], qkv_w_ref[...]).astype(LOW).astype(WIDE)
@@ -351,10 +351,13 @@
             ref[:, part * D : part * D + D] = jnp.concatenate(both, axis=0).astype(LOW)
 
 
-def table_sums(pair_ref, place_ref, turned):
+def turn(pair_ref, turned):
     for head in range(HEADS):
         turned[:, head, :] = pair_ref[head]
     turned[:, HEADS:ROWS, :] = jnp.zeros((TOK, ROWS - HEADS, TOK), WIDE)
+
+
+def table_sums(first, last, total, place_ref, turned):
     lane_at = lax.broadcasted_iota(jnp.int32, (LANES, TOK), 0)
 
     def step(block, total):
@@ -368,28 +371,52 @@
             total = total + nt(spread.astype(LOW), hot)
         return total
 
-    return lax.fori_loop(0, TOK // 8, step, jnp.zeros((CHUNKS * ROWS, LANES), WIDE))
-
-
-def finish_kernel(
+    return lax.fori_loop(first, last, step, total)
+
+
+def block_kernel(
     lat_count,
     lon_count,
-    y0,
-    y1,
-    y2,
-    y3,
-    terms_ref,
-    vgrad_ref,
-    pair_ref,
-    place_ref,
+    mask_ref,
+    fields_hbm,
+    cot_hbm,
+    table_hbm,
+    index_hbm,
+    qkv_w_hbm,
+    out_w_hbm,
+    token_ref,
+    gain_ref,
     output_ref,
     grad_ref,
     rows_ref,
     table_ref,
     vector_ref,
+    fields_v,
+    cot_v,
+    table_v,
+    index_v,
+    qkv_w_v,
+    out_w_v,
+    load_sem,
+    spread,
+    held,
+    leaving,
+    arrived,
+    padded_table,
+    packed_ref,
+    in_send,
+    in_recv,
+    bias_ref,
+    place_ref,
+    ys,
+    terms_ref,
+    vgrad_ref,
+    pair_ref,
+    qkv_s,
+    gm_s,
+    mixed_s,
+    gqkv_s,
     landed,
-    held,
-    spread,
     turned,
     pair_in,
     pair_sum,
@@ -431,12 +458,84 @@
     friends += [(lat_at(1), lon_at(1)), (lat_at(-1), lon_at(-1))]
     for friend in friends:
         pl.semaphore_signal(barrier, inc=1, device_id=friend, device_id_type=pl.DeviceIdType.MESH)
-    pl.semaphore_wait(barrier, len(friends))
-
-    pair_copy = remote(
-        terms_ref.at[:, :, 1 - core], pair_in, pair_send, pair_recv, (lat, lon + 1 - 2 * core)
+    pairs = (
+        (fields_hbm, fields_v),
+        (cot_hbm, cot_v),
+        (table_hbm, table_v),
+        (index_hbm, index_v),
+        (qkv_w_hbm, qkv_w_v),
+        (out_w_hbm, out_w_v),
     )
-    pair_copy.start()
+    loads = [pltpu.make_async_copy(src, dst, load_sem.at[i]) for i, (src, dst) in enumerate(pairs)]
+    for each in loads:
+        each.start()
+
+    in_copies = enter(
+        [(lat_at(-1), lon_at(-1)), (lat_at(-1), lon), (lat, lon_at(-1))],
+        loads,
+        mask_ref,
+        fields_v,
+        cot_v,
+        table_v,
+        index_v,
+        bias_ref,
+        place_ref,
+        spread,
+        held,
+        leaving,
+        arrived,
+        padded_table,
+        packed_ref,
+        in_send,
+        in_recv,
+        lambda: pl.semaphore_wait(barrier, len(friends)),
+    )
+    loads[4].wait()
+    loads[5].wait()
+    y0, y1, y2, y3 = (ys.at[i] for i in range(4))
+    attend(
+        lat_count,
+        lon_count,
+        lat == lat_count - 1,
+        leaving.at[3],
+        arrived.at[2],
+        arrived.at[1],
+        arrived.at[0],
+        token_ref,
+        gain_ref,
+        qkv_w_v,
+        out_w_v,
+        bias_ref,
+        y0,
+        y1,
+        y2,
+        y3,
+        terms_ref,
+        vgrad_ref,
+        pair_ref,
+        qkv_s,
+        gm_s,
+        mixed_s,
+        gqkv_s,
+    )
+
+    members = lat_count // 2
+    mine = (lat // 2 + lat) % 2
+    halves = (1 - mine, mine)
+    spans = [pl.ds(h * members, members) for h in halves]
+
+    pair_copies = [
+        remote(
+            terms_ref.at[span, :, 1 - core],
+            pair_in.at[span],
+            pair_send.at[i],
+            pair_recv.at[i],
+            (lat, lon + 1 - 2 * core),
+        )
+        for i, span in enumerate(spans)
+    ]
+    for each in pair_copies:
+        each.start()
     quads = [
         remote(y3, landed.at[0], quad_send.at[0], quad_recv.at[0], (lat_at(1), lon_at(1))),
         remote(y2, landed.at[1], quad_send.at[1], quad_recv.at[1], (lat_at(1), lon)),
@@ -452,26 +551,64 @@
     for each in vecs:
         each.start()
 
-    pair_copy.wait_recv()
-
-    def add_pair(row, carry):
-        for m in range(half):
-            own = terms_ref[row, m, core].astype(WIDE)
-            pair_sum[m, row] = (own + pair_in[row, m].astype(WIDE)).astype(LOW)
-        return carry
-
-    lax.fori_loop(0, lat_count, add_pair, 0)
-
+    turn(pair_ref, turned)
     lon_copies = []
-    for d in range(1, half):
-        to = (column + d) % half
-        lon_copies.append(
-            remote(pair_sum.at[to], lon_in.at[column], lon_send.at[to], lon_recv.at[column], (lat, 2 * to + core))
-        )
-    for each in lon_copies:
-        each.start()
-
-    total = table_sums(pair_ref, place_ref, turned)
+    for i in range(2):
+        pair_copies[i].wait_recv()
+
+        def add_pair(step, carry, base=halves[i] * members):
+            row = base + step
+            for m in range(half):
+                own = terms_ref[row, m, core].astype(WIDE)
+                pair_sum[m, row] = (own + pair_in[row, m].astype(WIDE)).astype(LOW)
+            return carry
+
+        lax.fori_loop(0, members, add_pair, 0)
+        for d in range(1, half):
+            to = (column + d) % half
+            each = remote(
+                pair_sum.at[to, spans[i]],
+                lon_in.at[column, spans[i]],
+                lon_send.at[i, to],
+                lon_recv.at[i, column],
+                (lat, 2 * to + core),
+            )
+            each.start()
+            lon_copies.append(each)
+
+    total = jnp.zeros((CHUNKS * ROWS, LANES), WIDE)
+    lat_copies = []
+    for i in range(2):
+        total = table_sums(8 * i, 8 * i + 8, total, place_ref, turned)
+        for d in range(1, half):
+            source = (column + d) % half
+            remote(
+                pair_sum.at[source, spans[i]],
+                lon_in.at[source, spans[i]],
+                lon_send.at[i, source],
+                lon_recv.at[i, source],
+                (lat, 2 * source + core),
+            ).wait_recv()
+
+        def add_lon(step, carry, base=halves[i] * members):
+            row = base + step
+            value = pair_sum[column, row].astype(WIDE)
+            for d in range(1, half):
+                value = value + lon_in[(column + d) % half, row].astype(WIDE)
+            lon_sum[row] = value.astype(LOW)
+            return carry
+
+        lax.fori_loop(0, members, add_lon, 0)
+        for d in range(i, members):
+            group = (lat // 2 + d) % members
+            to = 2 * group + (group + halves[i]) % 2
+            each = remote(
+                lon_sum.at[halves[i] * members + group], lat_in.at[lat], lat_send.at[to], lat_recv.at[lat], (to, lon)
+            )
+            each.start()
+            lat_copies.append(each)
+
+    total = table_sums(16, TOK // 8, total, place_ref, turned)
     for c in range(CHUNKS):
         table_in[lon, :, c * LANES : c * LANES + LANES] = total[c * ROWS : c * ROWS + ROWS].astype(LOW)
     tables = []
@@ -479,26 +616,6 @@
         to = lon_at(d)
         tables.append(remote(table_in.at[lon], table_in.at[lon], table_send.at[to], table_recv.at[lon], (lat, to)))
     for each in tables:
-        each.start()
-
-    for d in range(1, half):
-        source = (column + d) % half
-        remote(pair_sum.at[source], lon_in.at[source], lon_send.at[source], lon_recv.at[source], (lat, 2 * source + core)).wait_recv()
-
-    def add_lon(row, carry):
-        value = pair_sum[column, row].astype(WIDE)
-        for d in range(1, half):
-            value = value + lon_in[(column + d) % half, row].astype(WIDE)
-        lon_sum[row] = value.astype(LOW)
-        return carry
-
-    lax.fori_loop(0, lat_count, add_lon, 0)
-
-    lat_copies = []
-    for d in range(1, lat_count):
-        to = lat_at(d)
-        lat_copies.append(remote(lon_sum.at[to], lat_in.at[lat], lat_send.at[to], lat_recv.at[lat], (to, lon)))
-    for each in lat_copies:
         each.start()
 
     for d in range(1, lon_count):
@@ -544,15 +661,24 @@
         vec = vec + vec_in_lat[source]
     vector_ref[...] = vec[0:2]
 
-    value = lon_sum[lat].astype(WIDE)
+    value = lon_sum[position(lat, lat_count)].astype(WIDE)
     for d in range(1, lat_count):
         source = lat_at(d)
-        remote(lon_sum.at[source], lat_in.at[source], lat_send.at[source], lat_recv.at[source], (source, lon)).wait_recv()
+        remote(lon_sum.at[0], lat_in.at[source], lat_send.at[source], lat_recv.at[source], (source, lon)).wait_recv()
         value = value + lat_in[source].astype(WIDE)
     rows_ref[...] = value
 
-    for each in [pair_copy] + quads + vecs + lon_copies + tables + lat_copies + vec_lats:
+    for each in in_copies + pair_copies + quads + vecs + lon_copies + tables + lat_copies + vec_lats:
         each.wait_send()
+
+
+def write_kernel(*refs):
+    sems = refs[10]
+    copies = [pltpu.make_async_copy(refs[i], refs[5 + i], sems.at[i]) for i in range(5)]
+    for each in copies:
+        each.start()
+    for each in copies:
+        each.wait()
 
 
 def struct(shape, dtype):
@@ -570,66 +696,21 @@
     bias_table,
     bias_index,
 ):
-    quad = struct((QUAD, 2 * D), LOW)
     lat_count, lon_count = lax.axis_size("lat"), lax.axis_size("lon")
-    q0, q1, q2, q3, bias, place = pl.pallas_call(
-        functools.partial(enter_kernel, lat_count, lon_count),
-        out_shape=(quad,) * 4
-        + (struct((HEADS, TOK, 2 * LANES), WIDE), struct((TOK, 2 * LANES), jnp.int32)),
-        in_specs=[SMEM] + [VMEM] * 4,
-        out_specs=(VMEM,) * 6,
-        scratch_shapes=[
-            pltpu.VMEM((2, 3, 288, LANES), WIDE),
-            pltpu.VMEM((4, QUAD, 2 * D), WIDE),
-            pltpu.VMEM((3, QUAD, 2 * D), LOW),
-            pltpu.VMEM((3, QUAD, 2 * D), LOW),
-            pltpu.VMEM((ROWS, CHUNKS * LANES), WIDE),
-            pltpu.VMEM((PADDED, LANES), jnp.int32),
-            pltpu.SemaphoreType.DMA((3,)),
-            pltpu.SemaphoreType.DMA((3,)),
-        ],
-        compiler_params=pltpu.CompilerParams(
-            collective_id=1, has_side_effects=True, vmem_limit_bytes=32 * 1024 * 1024
-        ),
-        name="enter",
-    )(
-        window_mask.transpose(1, 2, 0),
-        fields.transpose(1, 2, 0, 3),
-        cotangent.transpose(1, 2, 0, 3),
-        bias_table.transpose(1, 0, 2),
-        bias_index,
-    )
-    edge = (lax.axis_index("lat") == lax.axis_size("lat") - 1).astype(jnp.int32).reshape(1)
-    y0, y1, y2, y3, wgrad, vgrad, pair = pl.pallas_call(
-        window_kernel,
-        out_shape=(quad,) * 4
-        + (struct((4 * D, D), LOW), struct((8, D), WIDE), struct((HEADS, TOK, TOK), WIDE)),
-        in_specs=[SMEM] + [VMEM] * 9,
-        out_specs=(VMEM,) * 7,
-        scratch_shapes=[
-            pltpu.VMEM((2 * TOK, 3 * D), LOW),
-            pltpu.VMEM((2 * TOK, D), LOW),
-            pltpu.VMEM((2 * TOK, D), LOW),
-            pltpu.VMEM((2 * TOK, 3 * D), LOW),
-        ],
-        compiler_params=PARAMS,
-        name="windows",
-    )(
-        edge,
-        q0,
-        q1,
-        q2,
-        q3,
-        mask_token.reshape(1, D),
-        norm_gain.reshape(1, D),
-        qkv_weight,
-        out_weight,
-        bias,
-    )
     half = lon_count // 2
     share = 4 * D // (lat_count * lon_count)
+
+    def low(*shape):
+        return pltpu.VMEM(shape, LOW)
+
+    def wide(*shape):
+        return pltpu.VMEM(shape, WIDE)
+
+    def sems(*shape):
+        return [pltpu.SemaphoreType.DMA(shape)] * 2
+
     output, input_grad, weight_grads, table_grad, vector_grads = pl.pallas_call(
-        functools.partial(finish_kernel, lat_count, lon_count),
+        functools.partial(block_kernel, lat_count, lon_count),
         out_shape=(
             struct((6, 12, 4, D), LOW),
             struct((6, 12, 4, D), LOW),
@@ -637,42 +718,77 @@
             struct((HEADS, 1, NBIAS), WIDE),
             struct((2, D), WIDE),
         ),
-        in_specs=[VMEM] * 8,
+        in_specs=[SMEM] + [HBM] * 6 + [VMEM] * 2,
         out_specs=(VMEM,) * 5,
         scratch_shapes=[
-            pltpu.VMEM((3, QUAD, 2 * D), LOW),
-            pltpu.VMEM((4, QUAD, 2 * D), WIDE),
-            pltpu.VMEM((2, 3, 288, LANES), WIDE),
-            pltpu.VMEM((TOK, ROWS, TOK), WIDE),
-            pltpu.VMEM((lat_count, half, share, D), LOW),
-            pltpu.VMEM((half, lat_count, share, D), LOW),
-            pltpu.VMEM((half, lat_count, share, D), LOW),
-            pltpu.VMEM((lat_count, share, D), LOW),
-            pltpu.VMEM((lat_count, share, D), LOW),
-            pltpu.VMEM((lon_count, ROWS, CHUNKS * LANES), LOW),
-            pltpu.VMEM((lon_count, 8, D), WIDE),
-            pltpu.VMEM((8, D), WIDE),
-            pltpu.VMEM((lat_count, 8, D), WIDE),
-            pltpu.SemaphoreType.DMA((3,)),
-            pltpu.SemaphoreType.DMA((3,)),
-            pltpu.SemaphoreType.DMA,
-            pltpu.SemaphoreType.DMA,
-            pltpu.SemaphoreType.DMA((half,)),
-            pltpu.SemaphoreType.DMA((half,)),
-            pltpu.SemaphoreType.DMA((lat_count,)),
-            pltpu.SemaphoreType.DMA((lat_count,)),
-            pltpu.SemaphoreType.DMA((lon_count,)),
-            pltpu.SemaphoreType.DMA((lon_count,)),
-            pltpu.SemaphoreType.DMA((lon_count,)),
-            pltpu.SemaphoreType.DMA((lon_count,)),
-            pltpu.SemaphoreType.DMA((lat_count,)),
-            pltpu.SemaphoreType.DMA((lat_count,)),
+            low(6, 12, 4, D),
+            low(6, 12, 4, D),
+            wide(HEADS, 1, NBIAS),
+            pltpu.VMEM((144, 144), jnp.int32),
+            low(3 * D, D),
+            low(D, D),
+            pltpu.SemaphoreType.DMA((6,)),
+            wide(2, 3, 288, LANES),
+            wide(4, QUAD, 2 * D),
+            low(4, QUAD, 2 * D),
+            low(3, QUAD, 2 * D),
+            wide(ROWS, CHUNKS * LANES),
+            pltpu.VMEM((PADDED, LANES), jnp.int32),
+            *sems(3),
+            wide(HEADS, TOK, 2 * LANES),
+            pltpu.VMEM((TOK, 2 * LANES), jnp.int32),
+            low(4, QUAD, 2 * D),
+            low(lat_count, half, 2, share, D),
+            wide(8, D),
+            wide(HEADS, TOK, TOK),
+            low(2 * TOK, 3 * D),
+            low(2 * TOK, D),
+            low(2 * TOK, D),
+            low(2 * TOK, 3 * D),
+            low(3, QUAD, 2 * D),
+            wide(TOK, ROWS, TOK),
+            low(lat_count, half, share, D),
+            low(half, lat_count, share, D),
+            low(half, lat_count, share, D),
+            low(lat_count, share, D),
+            low(lat_count, share, D),
+            low(lon_count, ROWS, CHUNKS * LANES),
+            wide(lon_count, 8, D),
+            wide(8, D),
+            wide(lat_count, 8, D),
+            *sems(3),
+            *sems(2),
+            *sems(2, half),
+            *sems(lat_count),
+            *sems(lon_count),
+            *sems(lon_count),
+            *sems(lat_count),
         ],
         compiler_params=pltpu.CompilerParams(
-            collective_id=0, has_side_effects=True, vmem_limit_bytes=32 * 1024 * 1024
+            collective_id=0, has_side_effects=True, vmem_limit_bytes=LIMIT
         ),
-        name="finish",
-    )(y0, y1, y2, y3, wgrad.reshape(lat_count, half, 2, share, D), vgrad, pair, place)
+        name="block",
+    )(
+        window_mask.transpose(1, 2, 0),
+        fields.transpose(1, 2, 0, 3),
+        cotangent.transpose(1, 2, 0, 3),
+        bias_table.transpose(1, 0, 2),
+        bias_index,
+        qkv_weight,
+        out_weight,
+        mask_token,
+        norm_gain,
+    )
+    results = (output, input_grad, weight_grads, table_grad, vector_grads)
+    output, input_grad, weight_grads, table_grad, vector_grads = pl.pallas_call(
+        write_kernel,
+        out_shape=tuple(struct(each.shape, each.dtype) for each in results),
+        in_specs=[HBM] * 5,
+        out_specs=(HBM,) * 5,
+        scratch_shapes=[pltpu.SemaphoreType.DMA((5,))],
+        compiler_params=PARAMS,
+        name="write",
+    )(*results)
     output = output.transpose(2, 0, 1, 3)
     input_grad = input_grad.transpose(2, 0, 1, 3)
     table_grad = table_grad.transpose(1, 0, 2)

time: 64.3 us -> 66.1 us (1.028)
  Pallas kernels: 52.4 us -> 65.3 us
  local copies, waits for them, and re-layouts: 10.9 us -> 0 us
    pallas_call x3 -> x2, Pallas kernels: 52.4 us -> 65.3 us  [the longest x1 47.3 us: local(): pl.pallas_call(functools.partial(block_kernel, lat_count, lon_count), out...]
    unnamed x19 -> x0, local copies, waits for them, and re-layouts: 9.52 us -> none
    reshape x2 -> x0, local copies, waits for them, and re-layouts: 1.36 us -> none  [the longest x1 0.68 us: local(): mask_token.reshape(1, D)]
where the time goes in v4:
time: 66.1 us; the launch traced here: 65.9 us
  Pallas kernels  65.3 us (99%)
    pallas_call x1, Pallas kernels, local(): pl.pallas_call(functools.partial(block_kernel, lat_count, lon_count), out...  47.3 us
    pallas_call x1, Pallas kernels, local(): pl.pallas_call(write_kernel, out_shape=tuple((struct(each.shape, each.dty...  18 us

profile of v4, /device:TPU:0, one launch (start us, length us, event | category | flops | bytes accessed | tf_op | source)
XLA Modules:
  0.0 65.9 jit_solution(11762343530792501975)
XLA Ops:
  0.6 47.3 %block.1 = (bf16[6,12,4,384]{3,2,1,0:T(4,128)(2,1)}, bf16[6,12,4,384]{3,2,1,0:T(4,128)(2,1)}, f32[48,384]{1,0:T(8,128)}, f32[12,1,759]{2,1,0:T(1,128)}, f32[2,384]{1,0:T(2,128)}) custom-call(s32[1,1,2]{2,1,0:T(1,128)} %bitcast.10, bf16[6,12,4,384]{3,2,1,0:T(4,128)(2,1)} %bitcast.7, bf16[6,12,4,384]{3,2,1,0:T(4,128)(2,1)} %bitcast.8, f32[12,1,759]{2,1,0:T(1,128)} %bitcast.9, ...), custom_call_target="tpu_custom_call" | custom-call | tf_op jit(solution)/shard_map/block/pallas_call | solution.py:712
  47.9 18.0 %write.1 = (bf16[6,12,4,384]{3,2,1,0:T(4,128)(2,1)}, bf16[6,12,4,384]{3,2,1,0:T(4,128)(2,1)}, f32[48,384]{1,0:T(8,128)}, f32[12,1,759]{2,1,0:T(1,128)}, f32[2,384]{1,0:T(2,128)}) custom-call(bf16[6,12,4,384]{3,2,1,0:T(4,128)(2,1)} %get-tuple-element.15.refs_0_, bf16[6,12,4,384]{3,2,1,0:T(4,128)(2,1)} %get-tuple-element.16.refs_1_, ...), custom_call_target="tpu_custom_call" | custom-call | tf_op jit(solution)/shard_map/write/pallas_call | solution.py:783

commit v5 on v4

--- a/solution.py
+++ b/solution.py
@@ -673,11 +673,15 @@
 
 
 def write_kernel(*refs):
-    sems = refs[10]
-    copies = [pltpu.make_async_copy(refs[i], refs[5 + i], sems.at[i]) for i in range(5)]
-    for each in copies:
+    sources, targets, buffers, in_sems, out_sems = refs[:5], refs[5:10], refs[10:15], refs[15], refs[16]
+    reads = [pltpu.make_async_copy(sources[i], buffers[i], in_sems.at[i]) for i in range(5)]
+    writes = [pltpu.make_async_copy(buffers[i], targets[i], out_sems.at[i]) for i in range(5)]
+    for each in reads:
         each.start()
-    for each in copies:
+    for i in range(5):
+        reads[i].wait()
+        writes[i].start()
+    for each in writes:
         each.wait()
 
 
@@ -785,7 +789,7 @@
         out_shape=tuple(struct(each.shape, each.dtype) for each in results),
         in_specs=[HBM] * 5,
         out_specs=(HBM,) * 5,
-        scratch_shapes=[pltpu.SemaphoreType.DMA((5,))],
+        scratch_shapes=[pltpu.VMEM(each.shape, each.dtype) for each in results] + sems(5),
         compiler_params=PARAMS,
         name="write",
     )(*results)

time: 66.1 us -> 49.9 us (0.75)
  Pallas kernels: 65.3 us -> 49.1 us
    pallas_call x1, Pallas kernels: 18 us -> 1.85 us  [local(): pl.pallas_call(write_kernel, out_shape=tuple((struct(each.shape, each.dty...]
where the time goes in v5:
time: 49.9 us; the launch traced here: 49.8 us
  Pallas kernels  49.1 us (98%)
  between operations  0.64 us (1%)
    pallas_call x1, Pallas kernels, local(): pl.pallas_call(functools.partial(block_kernel, lat_count, lon_count), out...  47.3 us
    pallas_call x1, Pallas kernels, local(): pl.pallas_call(write_kernel, out_shape=tuple((struct(each.shape, each.dty...  1.85 us

profile of v5, /device:TPU:0, one launch (start us, length us, event | category | flops | bytes accessed | tf_op | source)
XLA Modules:
  0.0 49.8 jit_solution(13673445476736236841)
XLA Ops:
  0.6 47.3 %block.1 = (bf16[6,12,4,384]{3,2,1,0:T(4,128)(2,1)}, bf16[6,12,4,384]{3,2,1,0:T(4,128)(2,1)}, f32[48,384]{1,0:T(8,128)}, f32[12,1,759]{2,1,0:T(1,128)}, f32[2,384]{1,0:T(2,128)}) custom-call(s32[1,1,2]{2,1,0:T(1,128)} %bitcast.10, bf16[6,12,4,384]{3,2,1,0:T(4,128)(2,1)} %bitcast.7, bf16[6,12,4,384]{3,2,1,0:T(4,128)(2,1)} %bitcast.8, f32[12,1,759]{2,1,0:T(1,128)} %bitcast.9, ...), custom_call_target="tpu_custom_call" | custom-call | tf_op jit(solution)/shard_map/block/pallas_call | solution.py:716
  47.9 1.8 %write.1 = (bf16[6,12,4,384]{3,2,1,0:T(4,128)(2,1)}, bf16[6,12,4,384]{3,2,1,0:T(4,128)(2,1)}, f32[48,384]{1,0:T(8,128)}, f32[12,1,759]{2,1,0:T(1,128)}, f32[2,384]{1,0:T(2,128)}) custom-call(bf16[6,12,4,384]{3,2,1,0:T(4,128)(2,1)} %get-tuple-element.15.refs_0_, bf16[6,12,4,384]{3,2,1,0:T(4,128)(2,1)} %get-tuple-element.16.refs_1_, ...), custom_call_target="tpu_custom_call" | custom-call | tf_op jit(solution)/shard_map/write/pallas_call | solution.py:787
